TPU v7x, 128 devices: a whole 4x4x4 slice. The times are simulated.
128 devices in a mesh: dp: 16 (over y, x), expert: 8 (over z, core).
Axes of the slice: x: 4, y: 4, z: 4, core: 2. Of those that a mesh axis runs over, the one named last changes fastest.
Arguments:
- tokens: bfloat16 [16384, 4096], P(('dp', 'expert')), may hold values from -6 to 6
- cotangent: bfloat16 [16384, 4096], P(('dp', 'expert')), may hold values from -6 to 6
- chosen: int32 [128, 8, 4], P(('dp', 'expert')), may hold values from 0 to 127, as said below
- counts: int32 [128, 8], P(('dp', 'expert')), may hold values from 0 to 4, as said below
- gate_prob: bfloat16 [128, 8, 4], P(('dp', 'expert')), may hold values from 0.049804688 to 1
- w_gate: bfloat16 [8, 4096, 7168], P('expert', None, 'dp'), may hold values from -0.09375 to 0.09375
- w_up: bfloat16 [8, 4096, 7168], P('expert', None, 'dp'), may hold values from -0.09375 to 0.09375
- w_down: bfloat16 [8, 7168, 4096], P('expert', 'dp'), may hold values from -0.0625 to 0.0625
Outputs:
- combined: bfloat16 [16384, 4096], P(('dp', 'expert'))
- token_grad: bfloat16 [16384, 4096], P(('dp', 'expert'))
- prob_grad: bfloat16 [128, 8, 4], P(('dp', 'expert'))
- grad_gate: bfloat16 [8, 4096, 7168], P('expert', None, 'dp')
- grad_up: bfloat16 [8, 4096, 7168], P('expert', None, 'dp')
- grad_down: bfloat16 [8, 7168, 4096], P('expert', 'dp')
Inputs may be any that keep to these rules, and one draw needn't show every extreme that they name: The 4 entries of chosen[s, e] are distinct local token indices of shard s; only the first counts[s, e] are used. For every expert, counts over all 128 token shards sum to exactly 256; some shards give 4 tokens to an expert.
All inputs are finite; a program needn't handle non-finite values.
Results may differ from a plain program's by a relative error of at most 0.012.
Values may be sent and summed in bfloat16 or wider, within the bound.
A program may use at most 128 MiB of HBM per device.

v0:
```python
import jax
import jax.numpy as jnp
from jax import lax
from jax.sharding import PartitionSpec as P


def expert_pass(inputs, scaled, w_gate, w_up, w_down):
    pre_gate = jnp.dot(inputs, w_gate, preferred_element_type=jnp.float32)
    pre_up = jnp.dot(inputs, w_up, preferred_element_type=jnp.float32)
    sigmoid = jax.nn.sigmoid(pre_gate)
    swish = pre_gate * sigmoid
    swish_slope = sigmoid * (1.0 + pre_gate * (1.0 - sigmoid))
    hidden = (swish * pre_up).astype(jnp.bfloat16)
    expert_out = jnp.dot(hidden, w_down, preferred_element_type=jnp.float32)
    hidden_grad = lax.dot_general(
        scaled, w_down, (((1,), (1,)), ((), ())), preferred_element_type=jnp.float32
    )
    pre_gate_grad = (hidden_grad * pre_up * swish_slope).astype(jnp.bfloat16)
    pre_up_grad = (hidden_grad * swish).astype(jnp.bfloat16)
    grad_gate = lax.dot_general(
        inputs, pre_gate_grad, (((0,), (0,)), ((), ())), preferred_element_type=jnp.float32
    )
    grad_up = lax.dot_general(
        inputs, pre_up_grad, (((0,), (0,)), ((), ())), preferred_element_type=jnp.float32
    )
    grad_down = lax.dot_general(
        hidden, scaled, (((0,), (0,)), ((), ())), preferred_element_type=jnp.float32
    )
    row_grad = lax.dot_general(
        pre_gate_grad, w_gate, (((1,), (1,)), ((), ())), preferred_element_type=jnp.float32
    )
    row_grad = row_grad + lax.dot_general(
        pre_up_grad, w_up, (((1,), (1,)), ((), ())), preferred_element_type=jnp.float32
    )
    return (
        expert_out,
        row_grad,
        grad_gate.astype(jnp.bfloat16),
        grad_up.astype(jnp.bfloat16),
        grad_down.astype(jnp.bfloat16),
    )


def send_back(reduced_out, reduced_grad):
    return (
        lax.all_to_all(reduced_out, "expert", split_axis=1, concat_axis=0, tiled=True),
        lax.all_to_all(reduced_grad, "expert", split_axis=1, concat_axis=0, tiled=True),
    )


def per_device(tokens, cotangent, chosen, counts, gate_prob, w_gate, w_up, w_down):
    expert_size = lax.axis_size("expert")
    local_experts = w_gate.shape[0]
    experts_all = local_experts * expert_size
    model_dim = tokens.shape[1]
    chosen_here = chosen[0]
    slot_count = chosen_here.shape[1]
    slot_iota = lax.broadcasted_iota(jnp.int32, chosen_here.shape, 1)
    is_live = slot_iota < counts[0][:, None]
    weights = jnp.where(is_live, gate_prob[0], jnp.zeros((), jnp.bfloat16))
    flat_index = chosen_here.reshape(-1)
    sent_tokens = tokens[flat_index].reshape(experts_all, slot_count, model_dim)
    sent_cot = cotangent[flat_index].reshape(experts_all, slot_count, model_dim)
    part_tokens, part_cot, part_weights = (
        lax.all_to_all(sent_tokens, "expert", split_axis=0, concat_axis=1, tiled=True),
        lax.all_to_all(sent_cot, "expert", split_axis=0, concat_axis=1, tiled=True),
        lax.all_to_all(weights, "expert", split_axis=0, concat_axis=1, tiled=True),
    )
    got_tokens, got_cot, got_weights = (
        lax.all_gather(part_tokens, "dp", axis=1, tiled=True),
        lax.all_gather(part_cot, "dp", axis=1, tiled=True),
        lax.all_gather(part_weights, "dp", axis=1, tiled=True),
    )
    rows_in = got_tokens[0]
    cot_in = got_cot[0]
    row_weights = got_weights[0].astype(jnp.float32)
    scaled = (row_weights[:, None] * cot_in.astype(jnp.float32)).astype(jnp.bfloat16)
    results = expert_pass(rows_in, scaled, w_gate[0], w_up[0], w_down[0])
    out_list = [results[0]]
    grad_list = [results[1]]
    gate_grads = [results[2]]
    up_grads = [results[3]]
    down_grads = [results[4]]
    out_parts = jnp.stack(out_list)
    grad_parts = jnp.stack(grad_list)
    reduced_out, reduced_grad = (
        lax.psum_scatter(out_parts, "dp", scatter_dimension=1, tiled=True),
        lax.psum_scatter(grad_parts, "dp", scatter_dimension=1, tiled=True),
    )
    back_out, back_grad = send_back(reduced_out, reduced_grad)
    flat_out = back_out.reshape(experts_all * slot_count, model_dim)
    flat_grad = back_grad.reshape(experts_all * slot_count, model_dim)
    token_iota = lax.broadcasted_iota(jnp.int32, (flat_index.shape[0], tokens.shape[0]), 1)
    matches = flat_index[:, None] == token_iota
    weighted = jnp.where(matches, weights.reshape(-1, 1).astype(jnp.float32), jnp.float32(0.0))
    live_match = jnp.where(matches & is_live.reshape(-1, 1), jnp.float32(1.0), jnp.float32(0.0))
    combined = lax.dot_general(
        weighted,
        flat_out,
        (((0,), (0,)), ((), ())),
        precision=lax.Precision.HIGHEST,
        preferred_element_type=jnp.float32,
    )
    token_grad = lax.dot_general(
        live_match,
        flat_grad,
        (((0,), (0,)), ((), ())),
        precision=lax.Precision.HIGHEST,
        preferred_element_type=jnp.float32,
    )
    inner = jnp.sum(sent_cot.astype(jnp.float32) * back_out, axis=-1)
    prob_grad = jnp.where(is_live, inner, jnp.float32(0.0))
    return (
        combined.astype(jnp.bfloat16),
        token_grad.astype(jnp.bfloat16),
        prob_grad[None].astype(jnp.bfloat16),
        jnp.stack(gate_grads),
        jnp.stack(up_grads),
        jnp.stack(down_grads),
    )


def solution(mesh):
    in_specs = (
        P(("dp", "expert"), None),
        P(("dp", "expert"), None),
        P(("dp", "expert"), None, None),
        P(("dp", "expert"), None),
        P(("dp", "expert"), None, None),
        P("expert", None, "dp"),
        P("expert", None, "dp"),
        P("expert", "dp", None),
    )
    out_specs = (
        P(("dp", "expert"), None),
        P(("dp", "expert"), None),
        P(("dp", "expert"), None, None),
        P("expert", None, "dp"),
        P("expert", None, "dp"),
        P("expert", "dp", None),
    )
    return jax.shard_map(
        per_device, mesh=mesh, in_specs=in_specs, out_specs=out_specs, check_vma=False
    )
```

profile of v0, /device:TPU:1, one launch (start us, length us, event | category | flops | bytes accessed | tf_op | source)
XLA Modules:
  0.0 342.3 jit_solution(12624134257321654218)
XLA Ops:
  7.2 0.9 copy.24
  8.4 0.7 gather_fusion
  9.2 13.1 %all_to_all.55 = bf16[8,4,4096]{2,1,0:T(4,128)(2,1)S(1)} all-to-all(bf16[8,4,4096]{2,1,0:T(4,128)(2,1)S(1)} %reshape.226), channel_id=1, replica_groups=mesh['dp'=16,'expert'=8] {'expert'}, dimensions={0} | all-to-all | bytes 524288 | tf_op jit(solution)/shard_map/all_to_all | solution.py:65
  22.4 0.8 all_to_all.18
  23.2 0.7 gather_fusion.1
  24.0 9.9 %all_to_all.56 = bf16[8,4,4096]{2,1,0:T(4,128)(2,1)S(1)} all-to-all(bf16[8,4,4096]{2,1,0:T(4,128)(2,1)S(1)} %reshape.228), channel_id=1, replica_groups=mesh['dp'=16,'expert'=8] {'expert'}, dimensions={0} | all-to-all | bytes 524288 | tf_op jit(solution)/shard_map/all_to_all | solution.py:66
  34.0 0.8 all_to_all.23
  34.8 0.7 copy.28
  35.5 4.3 %all-to-all-start.2 = ((bf16[8,1,4]{2,1,0:T(2,128)(2,1)}), bf16[8,1,4]{2,1,0:T(2,128)(2,1)S(1)}, u32[]{:S(2)}, u32[]{:S(2)}) async-start(bf16[8,1,4]{2,1,0:T(2,128)(2,1)} %copy.28), calls=%async_computation.3 | async-start | bytes 8192 | tf_op jit(solution)/shard_map/all_to_all | solution.py:67
  39.8 0.6 dynamic-slice
  41.0 3.3 all-to-all-done.2
  44.6 33.9 %all-reduce = bf16[512]{0:T(512)(128)(2,1)S(1)} all-reduce(bf16[512]{0:T(512)(128)(2,1)S(1)} %dynamic-update-slice), channel_id=1, replica_groups=mesh['dp'=16,'expert'=8] {'dp'}, use_global_device_ids=true, to_apply=%add | all-reduce | flops 512 | bytes 2048
  78.6 5.5 %fusion.12 = f32[512,448]{0,1:T(8,128)S(1)} fusion(bf16[1,512,4096]{2,1,0:T(8,128)(2,1)} %all-gather.3.cloned.1.call-done, bf16[1,4096,448]{1,2,0:T(8,128)(2,1)} %param.14), kind=kOutput, calls=%fused_computation.21 | convolution fusion | flops 1879048192 | bytes 8781824 | tf_op jit(solution)/shard_map/dot_general | solution.py:9
  84.2 3.0 fusion.14
  87.2 41.6 %all-gather.5.cloned.1.call-done = bf16[1,512,4096]{2,1,0:T(8,128)(2,1)} async-done(((bf16[1,32,4096]{2,1,0:T(8,128)(2,1)}), bf16[1,512,4096]{2,1,0:T(8,128)(2,1)}) %all-gather.5.cloned.1.call-update) | async-done | bytes 4194320 | tf_op jit(solution)/shard_map/all_gather | solution.py:71
  128.8 6.1 %multiply_convert_fusion = (bf16[512,448]{0,1:T(8,128)(2,1)S(1)}, bf16[512,448]{0,1:T(8,128)(2,1)S(1)}, bf16[512,448]{0,1:T(8,128)(2,1)S(1)}) fusion(f32[512,448]{0,1:T(8,128)} %fusion.14, f32[512,448]{0,1:T(8,128)S(1)} %fusion.12, bf16[1,448,4096]{2,1,0:T(8,128)(2,1)} %param.15, bf16[1,512,4096]{2,1,0:T(8,128)(2,1)} %all-gather.5.cloned.1.call-done, ...), kind=kOutput, calls=%fused_computation.34 | convolution fusion | flops 1888780288 | bytes 11077632 | tf_op jit(solution)/shard_map/dot_general | solution.py:15
  134.9 5.6 %convolution_bitcast_fusion = f32[1,512,4096]{2,1,0:T(8,128)} fusion(bf16[512,448]{0,1:T(8,128)(2,1)S(1)} %get-tuple-element.26, bf16[1,448,4096]{2,1,0:T(8,128)(2,1)S(1)} %copy-done.4), kind=kOutput, calls=%fused_computation.8 | convolution fusion | flops 1879048192 | bytes 12517376 | tf_op jit(solution)/shard_map/dot_general | solution.py:14
  140.8 4.6 %fusion.22 = f32[512,4096]{1,0:T(8,128)S(1)} fusion(bf16[512,448]{0,1:T(8,128)(2,1)S(1)} %get-tuple-element.25, bf16[1,4096,448]{1,2,0:T(8,128)(2,1)} %param.13), kind=kOutput, calls=%fused_computation.31 | convolution fusion | flops 1879048192 | bytes 12517376 | tf_op jit(solution)/shard_map/dot_general | solution.py:29
  145.4 5.9 %add_bitcast_fusion = f32[1,512,4096]{2,1,0:T(8,128)} fusion(f32[512,4096]{1,0:T(8,128)S(1)} %fusion.22, bf16[512,448]{0,1:T(8,128)(2,1)S(1)} %get-tuple-element.24, bf16[1,4096,448]{1,2,0:T(8,128)(2,1)S(1)} %copy-done.3), kind=kOutput, calls=%fused_computation.7 | convolution fusion | flops 1881145344 | bytes 20905984 | tf_op jit(solution)/shard_map/dot_general | solution.py:32
  151.7 6.2 %fusion.3 = bf16[1,448,4096]{2,1,0:T(8,128)(2,1)} fusion(bf16[512,448]{0,1:T(8,128)(2,1)S(1)} %get-tuple-element.26, bf16[1,512,4096]{2,1,0:T(8,128)(2,1)} %all-gather.5.cloned.1.call-done, f32[512]{0:T(512)S(1)} %convert_element_type.106), kind=kOutput, calls=%fused_computation.12 | convolution fusion | flops 1887174656 | bytes 8325120 | tf_op jit(solution)/shard_map/dot_general | solution.py:26
  157.9 65.9 %reduce-scatter.3.cloned.1.call-done = f32[1,32,4096]{2,1,0:T(8,128)} async-done(((f32[1,512,4096]{2,1,0:T(8,128)}), f32[1,32,4096]{2,1,0:T(8,128)}) %reduce-scatter.3.cloned.1.call-update) | async-done | bytes 524304 | tf_op jit(solution)/shard_map/reduce_scatter | solution.py:87
  223.9 2.4 copy.27
  226.2 6.5 %all-to-all-start.1 = ((f32[1,32,4096]{2,0,1:T(1,128)}), f32[1,32,4096]{2,0,1:T(1,128)S(1)}, u32[]{:S(2)}, u32[]{:S(2)}) async-start(f32[1,32,4096]{2,0,1:T(1,128)} %copy.27), calls=%async_computation.2 | async-start | bytes 1048576 | tf_op jit(solution)/shard_map/all_to_all | solution.py:46
  232.8 6.1 %fusion.4 = bf16[1,4096,448]{1,2,0:T(8,128)(2,1)} fusion(bf16[512,448]{0,1:T(8,128)(2,1)S(1)} %get-tuple-element.25, bf16[1,512,4096]{2,1,0:T(8,128)(2,1)} %all-gather.3.cloned.1.call-done), kind=kOutput, calls=%fused_computation.13 | convolution fusion | flops 1880883200 | bytes 8323072 | tf_op jit(solution)/shard_map/dot_general | solution.py:20
  238.9 72.6 %reduce-scatter.5.cloned.1.call-done = f32[1,32,4096]{2,1,0:T(8,128)} async-done(((f32[1,512,4096]{2,1,0:T(8,128)}), f32[1,32,4096]{2,1,0:T(8,128)}) %reduce-scatter.5.cloned.1.call-update) | async-done | bytes 524304 | tf_op jit(solution)/shard_map/reduce_scatter | solution.py:88
  311.5 2.4 copy.29
  313.9 6.5 %all-to-all-start.4 = ((f32[1,32,4096]{2,0,1:T(1,128)}), f32[1,32,4096]{2,0,1:T(1,128)S(1)}, u32[]{:S(2)}, u32[]{:S(2)}) async-start(f32[1,32,4096]{2,0,1:T(1,128)} %copy.29), calls=%async_computation.6 | async-start | bytes 1048576 | tf_op jit(solution)/shard_map/all_to_all | solution.py:47
  320.5 6.2 %fusion.5 = bf16[1,4096,448]{1,2,0:T(8,128)(2,1)} fusion(bf16[512,448]{0,1:T(8,128)(2,1)S(1)} %get-tuple-element.24, bf16[1,512,4096]{2,1,0:T(8,128)(2,1)} %all-gather.3.cloned.1.call-done), kind=kOutput, calls=%fused_computation.14 | convolution fusion | flops 1880883200 | bytes 8323072 | tf_op jit(solution)/shard_map/dot_general | solution.py:23
  327.2 0.7 copy.31
  327.9 2.1 all-to-all-done.4
  329.9 2.9 convolution_convert_fusion.3
  332.8 2.9 convolution_convert_fusion.4
  (50 shorter events, 2.3 us)
Async XLA Ops:
  7.2 1.2 copy-start
  7.2 16.0 %copy-start.2 = (bf16[128,4096]{1,0:T(8,128)(2,1)S(1)}, bf16[128,4096]{1,0:T(8,128)(2,1)}, u32[]{:S(2)}) copy-start(bf16[128,4096]{1,0:T(8,128)(2,1)} %param.9) | copy-start | bytes 3145732
  7.2 71.4 %all-gather.3.cloned.1.call-start = ((), (), s32[]{:S(2)}) async-start(), calls=%async_computation.7 | async-start | bytes 4456448 | tf_op jit(solution)/shard_map/all_gather | solution.py:70
  8.4 26.4 %copy-start.6 = (bf16[1,8,4]{1,2,0:T(4,128)(2,1)S(1)}, bf16[1,8,4]{1,2,0:T(4,128)(2,1)}, u32[]{:S(2)}) copy-start(bf16[1,8,4]{1,2,0:T(4,128)(2,1)} %param.12) | copy-start | bytes 196
  8.4 26.4 %copy-start.7 = (s32[1,8]{1,0:T(1,128)S(1)}, s32[1,8]{1,0:T(1,128)}, u32[]{:S(2)}) copy-start(s32[1,8]{1,0:T(1,128)} %param.11) | copy-start | bytes 100
  8.4 31.3 %copy-start.9 = (u32[128]{0:T(128)S(1)}, u32[128]{0:T(128)}, u32[]{:S(2)}) copy-start(u32[128]{0:T(128)} %constant.19) | copy-start | bytes 1540
  23.1 105.6 %all-gather.5.cloned.1.call-start = ((), (), s32[]{:S(2)}) async-start(), calls=%async_computation.9 | async-start | bytes 4456448 | tf_op jit(solution)/shard_map/all_gather | solution.py:71
  35.5 8.8 %all-to-all-start.2 = ((bf16[8,1,4]{2,1,0:T(2,128)(2,1)}), bf16[8,1,4]{2,1,0:T(2,128)(2,1)S(1)}, u32[]{:S(2)}, u32[]{:S(2)}) async-start(bf16[8,1,4]{2,1,0:T(2,128)(2,1)} %copy.28), calls=%async_computation.3 | async-start | bytes 8192 | tf_op jit(solution)/shard_map/all_to_all | solution.py:67
  39.7 184.1 %reduce-scatter.3.cloned.1.call-start = ((), (), s32[]{:S(2)}) async-start(), calls=%async_computation.8 | async-start | bytes 8912896 | tf_op jit(solution)/shard_map/reduce_scatter | solution.py:87
  78.6 5.6 %copy-start.5 = (bf16[1,4096,448]{1,2,0:T(8,128)(2,1)S(1)}, bf16[1,4096,448]{1,2,0:T(8,128)(2,1)}, u32[]{:S(2)}) copy-start(bf16[1,4096,448]{1,2,0:T(8,128)(2,1)} %param.13) | copy-start | bytes 11010052
  78.6 5.6 %copy-start.8 = (bf16[1,512,4096]{2,1,0:T(8,128)(2,1)S(1)}, bf16[1,512,4096]{2,1,0:T(8,128)(2,1)}, u32[]{:S(2)}) copy-start(bf16[1,512,4096]{2,1,0:T(8,128)(2,1)} %all-gather.3.cloned.1.call-done) | copy-start | bytes 12582916
  128.8 6.1 %copy-start.4 = (bf16[1,448,4096]{2,1,0:T(8,128)(2,1)S(1)}, bf16[1,448,4096]{2,1,0:T(8,128)(2,1)}, u32[]{:S(2)}) copy-start(bf16[1,448,4096]{2,1,0:T(8,128)(2,1)} %param.15) | copy-start | bytes 11010052
  140.5 171.0 %reduce-scatter.5.cloned.1.call-start = ((), (), s32[]{:S(2)}) async-start(), calls=%async_computation.10 | async-start | bytes 8912896 | tf_op jit(solution)/shard_map/reduce_scatter | solution.py:88
  140.7 4.6 %copy-start.3 = (bf16[1,4096,448]{1,2,0:T(8,128)(2,1)S(1)}, bf16[1,4096,448]{1,2,0:T(8,128)(2,1)}, u32[]{:S(2)}) copy-start(bf16[1,4096,448]{1,2,0:T(8,128)(2,1)} %param.14) | copy-start | bytes 11010052
  226.2 87.7 %all-to-all-start.1 = ((f32[1,32,4096]{2,0,1:T(1,128)}), f32[1,32,4096]{2,0,1:T(1,128)S(1)}, u32[]{:S(2)}, u32[]{:S(2)}) async-start(f32[1,32,4096]{2,0,1:T(1,128)} %copy.27), calls=%async_computation.2 | async-start | bytes 1048576 | tf_op jit(solution)/shard_map/all_to_all | solution.py:46
  313.9 16.0 %all-to-all-start.4 = ((f32[1,32,4096]{2,0,1:T(1,128)}), f32[1,32,4096]{2,0,1:T(1,128)S(1)}, u32[]{:S(2)}, u32[]{:S(2)}) async-start(f32[1,32,4096]{2,0,1:T(1,128)} %copy.29), calls=%async_computation.6 | async-start | bytes 1048576 | tf_op jit(solution)/shard_map/all_to_all | solution.py:47
  320.5 15.3 %copy-start.1 = (bf16[128,4096]{1,0:T(8,128)(2,1)S(1)}, bf16[128,4096]{1,0:T(8,128)(2,1)}, u32[]{:S(2)}) copy-start(bf16[128,4096]{1,0:T(8,128)(2,1)} %param.8) | copy-start | bytes 3145732
Sparse Core Ops, SparseCore 0:
  23.3 51.7 all-gather.2
  77.7 50.9 all-gather.4
  140.6 83.1 reduce-scatter.2
  227.1 84.3 reduce-scatter.4
where the time goes:
time: 343 us; the launch traced here: 342 us
  waiting for transfers between devices  186 us (54%)
  blocking collectives  57 us (17%)
  matrix products  55.1 us (16%)
  starting transfers between devices  17.6 us (5%)
  between operations  14.6 us (4%)
  local copies, waits for them, and re-layouts  11.8 us (3%)
    reduce_scatter x1, waiting for transfers between devices, per_device(): lax.psum_scatter(grad_parts, 'dp', scatter_dimension=1, tiled=True)  72.6 us
    reduce_scatter x1, waiting for transfers between devices, per_device(): lax.psum_scatter(out_parts, 'dp', scatter_dimension=1, tiled=True)  65.9 us
    all_gather x1, waiting for transfers between devices, per_device(): lax.all_gather(part_cot, 'dp', axis=1, tiled=True)  41.6 us
    unnamed x1, blocking collectives  33.9 us
    all_to_all x1, blocking collectives, per_device(): lax.all_to_all(sent_tokens, 'expert', split_axis=0, concat_axis=1, tiled=...  13.1 us
    all_to_all x1, blocking collectives, per_device(): lax.all_to_all(sent_cot, 'expert', split_axis=0, concat_axis=1, tiled=True)  9.95 us
  transfers between devices with their start and end apart: 7, of which 5 were waited for; matrix products, arithmetic and copies ran while one was open for 14% of the time, Pallas kernels for 0%

commit v1 on v0

v1 whole, which is shorter than its diff:
```python
import functools

import jax
import jax.numpy as jnp
from jax import lax
from jax.experimental import pallas as pl
from jax.experimental.pallas import tpu as pltpu
from jax.sharding import PartitionSpec as P

MESH = pl.DeviceIdType.MESH
BF = jnp.bfloat16
F32 = jnp.float32

D = 4096
HID = 448
TOK = 128
EXP = 8
PL = 16
SIDE = 4
M = 4
ROWS = 16
LIVE = ROWS * PL
Q = D // 4
H = D // 2


def dot(a, b, contract):
    return lax.dot_general(
        a, b, (((contract[0],), (contract[1],)), ((), ())), preferred_element_type=F32
    )


def iota(shape, dim):
    return lax.broadcasted_iota(jnp.int32, shape, dim)


def lanes256(tile):
    return jnp.concatenate([tile, tile], axis=1)[0:1, :]


def main_kernel(
    pidx_ref, pw_ref, cnt_ref, tok_hbm, cot_hbm, wg_hbm, wu_hbm, wd_hbm,
    t_out, s_out, hid_ref, pgg_ref, pug_ref, zr_ref,
    x_in, wg, wu, wd, csend, crecv, lsend, lrecv,
    zsend, zrecv, xsend, xrecv, esend, erecv, zsback, zrback,
    tbuf, sbuf, po, pr, r1, r2, r3, r4, qmat, fmat,
    in_sem, w_sem, out_sem, c_ss, c_rs, l_ss, l_rs, z_ss, z_rs, x_ss, x_rs,
    e_ss, e_rs, b_ss, b_rs, ag_ss, ag_rs, rs_ss, rs_rs,
):
    dp = lax.axis_index("dp")
    ex = lax.axis_index("expert")
    x, y = dp % SIDE, dp // SIDE

    def at_z(k):
        return (ex + k) % EXP

    def at_p(k):
        return (dp + k) % PL

    loads = []
    for a, src in enumerate((tok_hbm, cot_hbm)):
        for q in range(4):
            loads.append(
                pltpu.make_async_copy(
                    src.at[:, pl.ds(q * Q, Q)], x_in.at[a * 4 + q], in_sem.at[a * 4 + q]
                )
            )
    for c in loads:
        c.start()
    barrier = pltpu.get_barrier_semaphore()

    def greet_z(k, _):
        pl.semaphore_signal(barrier, inc=1, device_id=(dp, at_z(k)), device_id_type=MESH)
        return 0

    def greet_p(k, _):
        pl.semaphore_signal(barrier, inc=1, device_id=(at_p(k), ex), device_id_type=MESH)
        return 0

    lax.fori_loop(1, EXP, greet_z, 0)
    lax.fori_loop(1, PL, greet_p, 0)
    wcopies = [
        pltpu.make_async_copy(src, dst, w_sem.at[i])
        for i, (src, dst) in enumerate(((wg_hbm, wg), (wu_hbm, wu), (wd_hbm, wd)))
    ]

    csend[...] = cnt_ref[...]
    pick = jnp.where(
        iota((256, 8 * TOK), 1) == pidx_ref[...], pw_ref[...], F32(0.0)
    ).astype(BF)
    for c in loads:
        c.wait()
    for c in wcopies:
        c.start()
    zsend[...] = (
        dot(pick, x_in[...].reshape(8 * TOK, Q), (1, 0)).astype(BF).reshape(EXP, 32, Q)
    )
    pl.semaphore_wait(barrier, EXP - 1 + PL - 1)

    def c_copy(k, src, dst, peer):
        return pltpu.make_async_remote_copy(
            src_ref=csend.at[src], dst_ref=crecv.at[dst], send_sem=c_ss.at[k],
            recv_sem=c_rs.at[k], device_id=(dp, peer), device_id_type=MESH,
        )

    def z_copy(k, src, dst, peer):
        return pltpu.make_async_remote_copy(
            src_ref=zsend.at[src], dst_ref=zrecv.at[dst], send_sem=z_ss.at[k],
            recv_sem=z_rs.at[k], device_id=(dp, peer), device_id_type=MESH,
        )

    def start_c(k, _):
        c_copy(k, at_z(k), ex, at_z(k)).start()
        return 0

    def start_z(k, _):
        z_copy(k, at_z(k), ex, at_z(k)).start()
        return 0

    lax.fori_loop(1, EXP, start_c, 0)
    lax.fori_loop(1, EXP, start_z, 0)
    crecv[ex] = csend[ex]
    zrecv[ex] = zsend[ex]

    def wait_c(k, _):
        c_copy(k, at_z(k), at_z(EXP - k), at_z(k)).wait_recv()
        return 0

    lax.fori_loop(1, EXP, wait_c, 0)

    total = crecv[0]
    for s in range(1, EXP):
        total = total + crecv[s]
    lsend[...] = total
    lrecv[dp] = total

    def l_copy(k, dst, peer):
        return pltpu.make_async_remote_copy(
            src_ref=lsend, dst_ref=lrecv.at[dst], send_sem=l_ss.at[k],
            recv_sem=l_rs.at[k], device_id=(peer, ex), device_id_type=MESH,
        )

    def start_l(k, _):
        l_copy(k, dp, at_p(k)).start()
        return 0

    def wait_l(k, _):
        l_copy(k, at_p(PL - k), at_p(k)).wait_recv()
        return 0

    lax.fori_loop(1, PL, start_l, 0)

    lane = iota((8, 256), 1)
    src = lane // 32
    prefix = jnp.zeros((8, 256), jnp.int32)
    own = jnp.zeros((8, 256), jnp.int32)
    for s in range(EXP):
        v = jnp.concatenate([crecv[s], crecv[s]], axis=1)
        prefix = prefix + jnp.where(src > s, v, 0)
        own = jnp.where(src == s, v, own)
    slot = lane % M
    rank = jnp.where(slot < own, prefix + slot, -1)[0:1, :]

    lax.fori_loop(1, PL, wait_l, 0)
    zero = jnp.zeros((8, 128), jnp.int32)
    before = zero
    col = lane // ROWS
    off_l = jnp.zeros((8, 256), jnp.int32)
    len_l = jnp.zeros((8, 256), jnp.int32)
    running = zero
    for i in range(PL):
        v = lrecv[i]
        off_l = jnp.where(col == i, jnp.concatenate([running, running], axis=1), off_l)
        len_l = jnp.where(col == i, jnp.concatenate([v, v], axis=1), len_l)
        before = before + jnp.where(i < dp, v, zero)
        running = running + v
    offset = lanes256(before)
    r_l = ((dp - off_l + 512) & (ROWS - 1)) + ROWS * (lane % 2)
    pos = jnp.where(r_l < len_l, (off_l + r_l) // ROWS, -1)[0:1, :]

    row = iota((256, 256), 0)
    clane = iota((256, 256), 1)
    want = ((row // ROWS - offset + 512) & (ROWS - 1)) + ROWS * (row % 2)
    same = ((row // 4) % 4 == (clane // 8) % 4) & ((row // 2) % 2 == (clane // 4) % 2)
    qmat[...] = jnp.where(same & (want == rank), F32(1.0), F32(0.0)).astype(BF)
    frow = iota((128, 256), 0)
    flane = iota((128, 256), 1)
    fsame = (frow // 64 == (flane // 2) % 2) & ((frow // 16) % 4 == (flane // 4) % 4)
    fmat[...] = jnp.where(fsame & (frow % 16 == pos), F32(1.0), F32(0.0)).astype(BF)

    def wait_z(k, _):
        z_copy(k, at_z(k), at_z(EXP - k), at_z(k)).wait_recv()
        return 0

    lax.fori_loop(1, EXP, wait_z, 0)
    xsend[...] = (
        dot(qmat[...], zrecv[...].reshape(256, Q), (1, 0)).astype(BF).reshape(PL, ROWS, Q)
    )

    def x_copy(k, src, dst, peer):
        return pltpu.make_async_remote_copy(
            src_ref=xsend.at[src], dst_ref=xrecv.at[dst], send_sem=x_ss.at[k],
            recv_sem=x_rs.at[k], device_id=(peer, ex), device_id_type=MESH,
        )

    def start_x(k, _):
        x_copy(k, at_p(k), dp, at_p(k)).start()
        return 0

    def wait_x(k, _):
        x_copy(k, at_p(k), at_p(PL - k), at_p(k)).wait_recv()
        return 0

    lax.fori_loop(1, PL, start_x, 0)
    xrecv[dp] = xsend[dp]
    lax.fori_loop(1, PL, wait_x, 0)
    mine = dot(fmat[...], xrecv[...].reshape(256, Q), (1, 0)).astype(BF)
    for q in range(4):
        tbuf[dp, :, pl.ds(q * Q, Q)] = mine[q * 16 : q * 16 + 16]
        sbuf[dp, :, pl.ds(q * Q, Q)] = mine[64 + q * 16 : 64 + q * 16 + 16]

    def up(v, o):
        return (v + o + SIDE) % SIDE

    def index(part, u, v):
        return v * SIDE + u if part == 0 else u * SIDE + v

    def device(part, du, dv):
        if part == 0:
            return (up(y, dv) * SIDE + up(x, du), ex)
        return (up(y, du) * SIDE + up(x, dv), ex)

    gathered = (tbuf, sbuf)
    uv = ((x, y), (y, x))
    sent = []

    def ag(part, ident, block, half, du, dv):
        ref = gathered[part].at[block]
        if half is not None:
            ref = ref.at[:, pl.ds(half * H, H)]
        return pltpu.make_async_remote_copy(
            src_ref=ref, dst_ref=ref, send_sem=ag_ss.at[part, ident],
            recv_sem=ag_rs.at[part, ident], device_id=device(part, du, dv), device_id_type=MESH,
        )

    def ag_send(*args):
        c = ag(*args)
        c.start()
        sent.append(c)

    sign = (1, -1)

    def block_of(part, o, ov):
        u, v = uv[part]
        return index(part, up(u, o), up(v, ov))

    def phase2(part, o):
        for d in range(2):
            ag_send(part, 4 + o * 4 + d, block_of(part, o, 0), None, 0, sign[d])

    def pass_on2(part, o):
        for d in range(2):
            b = block_of(part, o, -sign[d])
            ag(part, 4 + o * 4 + d, b, None, 0, sign[d]).wait_recv()
            ag_send(part, 4 + o * 4 + 2 + d, b, d, 0, sign[d])

    for part in range(2):
        for d in range(2):
            ag_send(part, d, block_of(part, 0, 0), None, sign[d], 0)
        phase2(part, 0)
    for part in range(2):
        for d in range(2):
            o = 3 if d == 0 else 1
            b = block_of(part, o, 0)
            ag(part, d, b, None, sign[d], 0).wait_recv()
            ag_send(part, 2 + d, b, d, sign[d], 0)
            phase2(part, o)
    for part in range(2):
        pass_on2(part, 0)
    for part in range(2):
        for d in range(2):
            ag(part, 2 + d, block_of(part, 2, 0), d, sign[d], 0).wait_recv()
        phase2(part, 2)
    for o in (3, 1, 2):
        for part in range(2):
            pass_on2(part, o)
    for o in (0, 3, 1, 2):
        for part in range(2):
            for d in range(2):
                ag(part, 4 + o * 4 + 2 + d, block_of(part, o, 2), d, 0, sign[d]).wait_recv()

    outs = [
        pltpu.make_async_copy(tbuf, t_out, out_sem.at[0]),
        pltpu.make_async_copy(sbuf, s_out, out_sem.at[1]),
    ]
    for c in outs:
        c.start()

    for c in wcopies:
        c.wait()
    rows_in = tbuf[...].reshape(LIVE, D)
    pre_gate = dot(rows_in, wg[...], (1, 0))
    pre_up = dot(rows_in, wu[...], (1, 0))
    hidden_grad = dot(sbuf[...].reshape(LIVE, D), wd[...], (1, 1))
    sig = jax.nn.sigmoid(pre_gate)
    swish = pre_gate * sig
    slope = sig * (1.0 + pre_gate * (1.0 - sig))
    hid_ref[...] = (swish * pre_up).astype(BF)
    pgg_ref[...] = (hidden_grad * pre_up * slope).astype(BF)
    pug_ref[...] = (hidden_grad * swish).astype(BF)

    partial = (po, pr)
    WIDE = 512

    def second(n, _):
        cols = pl.ds(pl.multiple_of(n * WIDE, WIDE), WIDE)
        po[:, :, :, cols] = (
            dot(hid_ref[...], wd[:, cols], (1, 0)).astype(BF).reshape(SIDE, SIDE, ROWS, WIDE)
        )
        grad = dot(pgg_ref[...], wg[cols, :], (1, 1)) + dot(pug_ref[...], wu[cols, :], (1, 1))
        pr[:, :, :, cols] = grad.astype(BF).reshape(SIDE, SIDE, ROWS, WIDE)
        return 0

    def cols_of(half):
        return pl.ds(half * H, H)

    def group(part, ov):
        v = up(uv[part][1], ov)
        return partial[part].at[v] if part == 0 else partial[part].at[:, v]

    def piece(part, ou):
        u, v = up(uv[part][0], ou), uv[part][1]
        return partial[part].at[v, u] if part == 0 else partial[part].at[u, v]

    def rs(part, ident, src, dst, du, dv):
        return pltpu.make_async_remote_copy(
            src_ref=src, dst_ref=dst, send_sem=rs_ss.at[part, ident],
            recv_sem=rs_rs.at[part, ident], device_id=device(part, du, dv), device_id_type=MESH,
        )

    def far(part, d):
        return rs(part, d, group(part, 2).at[:, :, cols_of(d)], r1.at[part, d], 0, sign[d])

    def near(part, d, h):
        return rs(
            part, 2 + 2 * d + h, group(part, sign[d]).at[:, :, cols_of(h)],
            r2.at[part, d, h], 0, sign[d],
        )

    def far1(part, d):
        return rs(part, 6 + d, piece(part, 2).at[:, cols_of(d)], r3.at[part, d], sign[d], 0)

    def near1(part, d, h):
        return rs(
            part, 8 + 2 * d + h, piece(part, sign[d]).at[:, cols_of(h)],
            r4.at[part, d, h], sign[d], 0,
        )

    def go(c):
        c.start()
        sent.append(c)

    for h in range(2):
        lax.fori_loop(h * 4, h * 4 + 4, second, 0)
        for part in range(2):
            go(far(part, h))
        for part in range(2):
            go(near(part, 1 - h, h))
    for d in range(2):
        for part in range(2):
            far(part, d).wait_recv()
            ref = group(part, sign[d]).at[:, :, cols_of(d)]
            ref[...] = (ref[...].astype(F32) + r1[part, d].astype(F32)).astype(BF)
            go(near(part, d, d))
    for part in range(2):
        for d in range(2):
            for h in range(2):
                near(part, d, h).wait_recv()
        for o in (2, 1, 3, 0):
            u = up(uv[part][0], o)
            for h in range(2):
                ref = piece(part, o).at[:, cols_of(h)]
                ref[...] = (
                    ref[...].astype(F32)
                    + r2[part, 0, h, u].astype(F32)
                    + r2[part, 1, h, u].astype(F32)
                ).astype(BF)
            if o == 2:
                go(far1(part, 0))
                go(far1(part, 1))
            elif o != 0:
                d = 0 if o == 1 else 1
                go(near1(part, d, 1 - d))
    for part in range(2):
        for d in range(2):
            far1(part, d).wait_recv()
            ref = piece(part, sign[d]).at[:, cols_of(d)]
            ref[...] = (ref[...].astype(F32) + r3[part, d].astype(F32)).astype(BF)
            go(near1(part, d, d))
    reduced = []
    for part in range(2):
        for h in range(2):
            for d in range(2):
                near1(part, d, h).wait_recv()
            full = (
                piece(part, 0)[:, cols_of(h)].astype(F32)
                + r4[part, 0, h].astype(F32)
                + r4[part, 1, h].astype(F32)
            ).astype(BF)
            reduced += [full[:, :Q], full[:, Q:]]

    esend[...] = (
        dot(fmat[...], jnp.concatenate(reduced, axis=0), (0, 0)).astype(BF).reshape(PL, ROWS, Q)
    )

    def e_copy(k, src, dst, peer):
        return pltpu.make_async_remote_copy(
            src_ref=esend.at[src], dst_ref=erecv.at[dst], send_sem=e_ss.at[k],
            recv_sem=e_rs.at[k], device_id=(peer, ex), device_id_type=MESH,
        )

    def start_e(k, _):
        e_copy(k, at_p(k), dp, at_p(k)).start()
        return 0

    def wait_e(k, _):
        e_copy(k, at_p(k), at_p(PL - k), at_p(k)).wait_recv()
        return 0

    lax.fori_loop(1, PL, start_e, 0)
    erecv[dp] = esend[dp]
    lax.fori_loop(1, PL, wait_e, 0)
    zsback[...] = (
        dot(qmat[...], erecv[...].reshape(256, Q), (0, 0)).astype(BF).reshape(EXP, 32, Q)
    )

    def b_copy(k, src, dst, peer):
        return pltpu.make_async_remote_copy(
            src_ref=zsback.at[src], dst_ref=zrback.at[dst], send_sem=b_ss.at[k],
            recv_sem=b_rs.at[k], device_id=(dp, peer), device_id_type=MESH,
        )

    def start_b(k, _):
        b_copy(k, at_z(k), ex, at_z(k)).start()
        return 0

    def wait_b(k, _):
        b_copy(k, at_z(k), at_z(EXP - k), at_z(k)).wait_recv()
        return 0

    lax.fori_loop(1, EXP, start_b, 0)
    zrback[ex] = zsback[ex]
    lax.fori_loop(1, EXP, wait_b, 0)
    zr_ref[...] = zrback[...].reshape(256, Q)

    def done_z(k, _):
        c_copy(k, at_z(k), ex, at_z(k)).wait_send()
        z_copy(k, at_z(k), ex, at_z(k)).wait_send()
        b_copy(k, at_z(k), ex, at_z(k)).wait_send()
        return 0

    def done_p(k, _):
        l_copy(k, dp, at_p(k)).wait_send()
        x_copy(k, at_p(k), dp, at_p(k)).wait_send()
        e_copy(k, at_p(k), dp, at_p(k)).wait_send()
        return 0

    lax.fori_loop(1, EXP, done_z, 0)
    lax.fori_loop(1, PL, done_p, 0)
    for c in sent:
        c.wait_send()
    for c in outs:
        c.wait()


def run_main(pidx, pw, cnt, tokens, cotangent, wg, wu, wd):
    vmem = pl.BlockSpec(memory_space=pltpu.VMEM)
    anym = pl.BlockSpec(memory_space=pl.ANY)
    dma = pltpu.SemaphoreType.DMA
    return pl.pallas_call(
        main_kernel,
        out_shape=(
            jax.ShapeDtypeStruct((PL, ROWS, D), BF),
            jax.ShapeDtypeStruct((PL, ROWS, D), BF),
            jax.ShapeDtypeStruct((LIVE, HID), BF),
            jax.ShapeDtypeStruct((LIVE, HID), BF),
            jax.ShapeDtypeStruct((LIVE, HID), BF),
            jax.ShapeDtypeStruct((256, Q), BF),
        ),
        in_specs=[vmem] * 3 + [anym] * 5,
        out_specs=(anym, anym, vmem, vmem, vmem, vmem),
        scratch_shapes=[
            pltpu.VMEM((8, TOK, Q), BF),
            pltpu.VMEM((D, HID), BF),
            pltpu.VMEM((D, HID), BF),
            pltpu.VMEM((HID, D), BF),
            pltpu.VMEM((EXP, 8, 128), jnp.int32),
            pltpu.VMEM((EXP, 8, 128), jnp.int32),
            pltpu.VMEM((8, 128), jnp.int32),
            pltpu.VMEM((PL, 8, 128), jnp.int32),
            pltpu.VMEM((EXP, 32, Q), BF),
            pltpu.VMEM((EXP, 32, Q), BF),
            pltpu.VMEM((PL, ROWS, Q), BF),
            pltpu.VMEM((PL, ROWS, Q), BF),
            pltpu.VMEM((PL, ROWS, Q), BF),
            pltpu.VMEM((PL, ROWS, Q), BF),
            pltpu.VMEM((EXP, 32, Q), BF),
            pltpu.VMEM((EXP, 32, Q), BF),
            pltpu.VMEM((PL, ROWS, D), BF),
            pltpu.VMEM((PL, ROWS, D), BF),
            pltpu.VMEM((SIDE, SIDE, ROWS, D), BF),
            pltpu.VMEM((SIDE, SIDE, ROWS, D), BF),
            pltpu.VMEM((2, 2, SIDE, ROWS, H), BF),
            pltpu.VMEM((2, 2, 2, SIDE, ROWS, H), BF),
            pltpu.VMEM((2, 2, ROWS, H), BF),
            pltpu.VMEM((2, 2, 2, ROWS, H), BF),
            pltpu.VMEM((256, 256), BF),
            pltpu.VMEM((128, 256), BF),
            dma((8,)),
            dma((3,)),
            dma((2,)),
            dma((EXP,)),
            dma((EXP,)),
            dma((PL,)),
            dma((PL,)),
            dma((EXP,)),
            dma((EXP,)),
            dma((PL,)),
            dma((PL,)),
            dma((PL,)),
            dma((PL,)),
            dma((EXP,)),
            dma((EXP,)),
            dma((2, 20)),
            dma((2, 20)),
            dma((2, 12)),
            dma((2, 12)),
        ],
        compiler_params=pltpu.CompilerParams(
            collective_id=0, has_side_effects=True, vmem_limit_bytes=58 * 1024 * 1024
        ),
        cost_estimate=pl.CostEstimate(
            flops=6 * 2 * LIVE * D * HID, bytes_accessed=20 << 20, transcendentals=LIVE * HID
        ),
        name="routed_experts",
    )(pidx, pw, cnt, tokens, cotangent, wg, wu, wd)


TILE = 512


def tail_kernel(
    cidx_ref, cw_ref, clive_ref, t_ref, s_ref, hid_ref, pgg_ref, pug_ref, zr_ref, cot_ref,
    comb_ref, tg_ref, prob_ref, gg_ref, gu_ref, gd_ref,
):
    step = pl.program_id(0)
    tile = t_ref[...]
    gg_ref[...] = dot(tile, pgg_ref[...], (0, 0)).astype(BF)
    gu_ref[...] = dot(tile, pug_ref[...], (0, 0)).astype(BF)
    gd_ref[...] = dot(hid_ref[...], s_ref[...], (0, 0)).astype(BF)

    q = step // (Q // TILE)
    r = iota((64, 256), 0)
    c = iota((64, 256), 1)
    target = (((r % 32) // 4) * 4 + q) * 8 + (r // 32) * 4 + r % 4
    rows = dot(jnp.where(c == target, F32(1.0), F32(0.0)).astype(BF), zr_ref[...], (1, 0))
    out_rows = rows[:32]
    grad_rows = rows[32:]
    match = iota((32, TOK), 1) == cidx_ref[...]
    pick_w = jnp.where(match, cw_ref[...], F32(0.0)).astype(BF)
    pick_live = jnp.where(match, clive_ref[...], F32(0.0)).astype(BF)
    comb_ref[...] = dot(pick_w, out_rows.astype(BF), (0, 0)).astype(BF)
    tg_ref[...] = dot(pick_live, grad_rows.astype(BF), (0, 0)).astype(BF)
    cot_rows = dot(pick_live, cot_ref[...], (1, 0))
    prod = cot_rows * out_rows
    part = prod[:, 0:128]
    for i in range(1, TILE // 128):
        part = part + prod[:, i * 128 : (i + 1) * 128]

    @pl.when(step == 0)
    def _():
        prob_ref[...] = jnp.zeros_like(prob_ref)

    prob_ref[...] += part


def run_tail(cidx, cw, clive, t, s, hid, pgg, pug, zr, cotangent):
    def whole(shape):
        return pl.BlockSpec(shape, lambda i: (0, 0))

    per_q = Q // TILE
    return pl.pallas_call(
        tail_kernel,
        grid=(D // TILE,),
        out_shape=(
            jax.ShapeDtypeStruct((TOK, D), BF),
            jax.ShapeDtypeStruct((TOK, D), BF),
            jax.ShapeDtypeStruct((32, 128), F32),
            jax.ShapeDtypeStruct((D, HID), BF),
            jax.ShapeDtypeStruct((D, HID), BF),
            jax.ShapeDtypeStruct((HID, D), BF),
        ),
        in_specs=[
            whole((32, 1)),
            whole((32, 1)),
            whole((32, 1)),
            pl.BlockSpec((LIVE, TILE), lambda i: (0, i)),
            pl.BlockSpec((LIVE, TILE), lambda i: (0, i)),
            whole((LIVE, HID)),
            whole((LIVE, HID)),
            whole((LIVE, HID)),
            pl.BlockSpec((256, TILE), lambda i: (0, i % per_q)),
            pl.BlockSpec((TOK, TILE), lambda i: (0, i)),
        ],
        out_specs=(
            pl.BlockSpec((TOK, TILE), lambda i: (0, i)),
            pl.BlockSpec((TOK, TILE), lambda i: (0, i)),
            whole((32, 128)),
            pl.BlockSpec((TILE, HID), lambda i: (i, 0)),
            pl.BlockSpec((TILE, HID), lambda i: (i, 0)),
            pl.BlockSpec((HID, TILE), lambda i: (0, i)),
        ),
        compiler_params=pltpu.CompilerParams(vmem_limit_bytes=40 * 1024 * 1024),
        cost_estimate=pl.CostEstimate(
            flops=3 * 2 * LIVE * D * HID, bytes_accessed=20 << 20, transcendentals=0
        ),
        name="weight_grads_and_combine",
    )(cidx, cw, clive, t, s, hid, pgg, pug, zr, cotangent)


def per_device(tokens, cotangent, chosen, counts, gate_prob, w_gate, w_up, w_down):
    chosen_here = chosen[0]
    slot_iota = lax.broadcasted_iota(jnp.int32, (EXP, M), 1)
    is_live = slot_iota < counts[0][:, None]
    weights = jnp.where(is_live, gate_prob[0].astype(F32), F32(0.0))
    piece = lax.broadcasted_iota(jnp.int32, (EXP, 4, 2, M), 1)
    array = lax.broadcasted_iota(jnp.int32, (EXP, 4, 2, M), 2)
    pidx = ((array * 4 + piece) * TOK + chosen_here[:, None, None, :]).reshape(256, 1)
    pw = jnp.where(array == 0, F32(1.0), weights[:, None, None, :]).reshape(256, 1)
    cnt = jnp.broadcast_to(counts[0][:, None, None], (EXP, 8, 128))
    t, s, hid, pgg, pug, zr = run_main(
        pidx, pw, cnt, tokens, cotangent, w_gate[0], w_up[0], w_down[0]
    )
    combined, token_grad, prob, gg, gu, gd = run_tail(
        chosen_here.reshape(32, 1),
        weights.reshape(32, 1),
        is_live.astype(F32).reshape(32, 1),
        t.reshape(LIVE, D),
        s.reshape(LIVE, D),
        hid,
        pgg,
        pug,
        zr,
        cotangent,
    )
    inner = jnp.sum(prob, axis=-1).reshape(EXP, M)
    prob_grad = jnp.where(is_live, inner, F32(0.0)).astype(BF)
    return combined, token_grad, prob_grad[None], gg[None], gu[None], gd[None]


def solution(mesh):
    tokens = P(("dp", "expert"), None)
    slots = P(("dp", "expert"), None, None)
    specs = (tokens, tokens, slots, tokens, slots)
    weights = (P("expert", None, "dp"), P("expert", None, "dp"), P("expert", "dp", None))
    return jax.shard_map(
        per_device,
        mesh=mesh,
        in_specs=specs + weights,
        out_specs=(tokens, tokens, slots) + weights,
        check_vma=False,
    )
```

time: 343 us -> 158 us (0.46)
  waiting for transfers between devices: 186 us -> 0 us
  Pallas kernels: 0 us -> 114 us
  blocking collectives: 57 us -> 0 us
  matrix products: 55.1 us -> 0 us
  local copies, waits for them, and re-layouts: 11.8 us -> 40.9 us
  starting transfers between devices: 17.6 us -> 0 us
  between operations: 14.6 us -> 0.7 us
    reduce_scatter x2 -> x0, waiting for transfers between devices: 139 us -> none  [the longest x1 72.6 us: per_device(): lax.psum_scatter(grad_parts, 'dp', scatter_dimension=1, tiled=True)]
    pallas_call x0 -> x2, Pallas kernels: none -> 114 us  [the longest x1 105 us: run_main(): pl.pallas_call(main_kernel, out_shape=(jax.ShapeDtypeStruct((PL, ROWS, D)...]
    dot_general x11 -> x0, matrix products: 55.1 us -> none  [the longest x1 6.22 us: expert_pass(): lax.dot_general(hidden, scaled, (((0,), (0,)), ((), ())), preferred_eleme...]
    all_gather x2 -> x0, waiting for transfers between devices: 41.6 us -> none  [the longest x1 41.6 us: per_device(): lax.all_gather(part_cot, 'dp', axis=1, tiled=True)]
    unnamed x1 -> x0, blocking collectives: 33.9 us -> none
    unnamed x27 -> x24, local copies, waits for them, and re-layouts: 2.84 us -> 35.8 us
    all_to_all x2 -> x0, blocking collectives: 23.1 us -> none  [the longest x1 13.1 us: per_device(): lax.all_to_all(sent_tokens, 'expert', split_axis=0, concat_axis=1, tiled=...]
    all_to_all x3 -> x0, starting transfers between devices: 17.3 us -> none  [the longest x1 6.55 us: send_back(): lax.all_to_all(reduced_grad, 'expert', split_axis=1, concat_axis=0, tiled...]
  transfers between devices with their start and end apart: 7 -> 0, of which waited for: 5 -> 0; matrix products, arithmetic and copies ran while one was open for 14% -> 0% of each run, Pallas kernels for 0% -> 0%
where the time goes in v1:
time: 158 us; the launch traced here: 157 us
  Pallas kernels  114 us (72%)
  local copies, waits for them, and re-layouts  40.9 us (26%)
  other arithmetic  1.72 us (1%)
    pallas_call x1, Pallas kernels, run_main(): pl.pallas_call(main_kernel, out_shape=(jax.ShapeDtypeStruct((PL, ROWS, D)...  105 us
    unnamed x24, local copies, waits for them, and re-layouts  35.8 us
    pallas_call x1, Pallas kernels, run_tail(): pl.pallas_call(tail_kernel, grid=(D // TILE,), out_shape=(jax.ShapeDtypeS...  8.54 us

profile of v1, /device:TPU:1, one launch (start us, length us, event | category | flops | bytes accessed | tf_op | source)
XLA Modules:
  0.0 157.2 jit_solution(2726272693745112882)
XLA Ops:
  0.6 0.7 iota_compare_fusion.1
  1.3 0.1 copy.45
  1.4 0.1 lt.42
  1.5 0.7 bitcast_select_fusion
  2.2 0.1 copy.50
  2.3 0.1 copy.47
  2.4 0.8 copy.49
  3.1 0.8 copy.44
  3.9 0.8 copy.46
  4.7 0.1 reshape.217
  4.8 0.1 copy.56.clive_ref
  4.9 0.1 multiply_add_fusion
  5.0 0.1 broadcast_select_fusion
  5.1 1.3 broadcast_in_dim.41.cnt_ref
  6.4 0.8 select_n.46.pw_ref
  7.2 0.8 add.36.pidx_ref
  8.0 6.4 %copy.51 = bf16[1,4096,448]{2,1,0:T(8,128)(2,1)} copy(bf16[1,4096,448]{1,2,0:T(8,128)(2,1)} %param.13) | data formatting | bytes 7340032 | tf_op args[5]
  14.3 6.4 %copy.52 = bf16[1,4096,448]{2,1,0:T(8,128)(2,1)} copy(bf16[1,4096,448]{1,2,0:T(8,128)(2,1)} %param.14) | data formatting | bytes 7340032 | tf_op args[6]
  20.8 105.3 %routed_experts.1 = (bf16[16,16,4096]{2,1,0:T(8,128)(2,1)}, bf16[16,16,4096]{2,1,0:T(8,128)(2,1)}, bf16[256,448]{1,0:T(8,128)(2,1)}, bf16[256,448]{1,0:T(8,128)(...) custom-call(s32[256,1]{1,0:T(8,128)} %add.36.pidx_ref, f32[256,1]{1,0:T(8,128)} %select_n.46.pw_ref, ...), custom_call_target="tpu_custom_call" | custom-call | flops 5637144576 | bytes 20971520 | tf_op jit(solution)/shard_map/routed_experts/pallas_call | solution.py:480
  126.1 1.6 %copy-done.2 = bf16[16,16,4096]{2,1,0:T(8,128)(2,1)S(1)} copy-done((bf16[16,16,4096]{2,1,0:T(8,128)(2,1)S(1)}, bf16[16,16,4096]{2,1,0:T(8,128)(2,1)}, u32[]{:S(2)}) %copy-start.2) | copy-done | bytes 2097176
  127.7 1.6 %copy-done.3 = bf16[16,16,4096]{2,1,0:T(8,128)(2,1)S(1)} copy-done((bf16[16,16,4096]{2,1,0:T(8,128)(2,1)S(1)}, bf16[16,16,4096]{2,1,0:T(8,128)(2,1)}, u32[]{:S(2)}) %copy-start.3) | copy-done | bytes 2097176
  129.3 1.0 copy-done.4
  130.3 0.9 copy-done.5
  131.3 0.9 copy-done.6
  132.2 0.9 copy-done.7
  133.2 8.5 %weight_grads_and_combine.1 = (bf16[128,4096]{1,0:T(8,128)(2,1)}, bf16[128,4096]{1,0:T(8,128)(2,1)}, f32[32,128]{1,0:T(8,128)S(1)}, bf16[4096,448]{1,0:T(8,128)(...) custom-call(s32[32,1]{1,0:T(8,128)S(1)} %reshape_squeeze.4.cidx_ref, ...), custom_call_target="tpu_custom_call" | custom-call | flops 2818572288 | bytes 20971520 | tf_op jit(solution)/shard_map/weight_grads_and_combine/pallas_call | solution.py:592
  141.7 2.0 %copy-done = bf16[4096,448]{1,0:T(8,128)(2,1)} copy-done((bf16[4096,448]{1,0:T(8,128)(2,1)}, bf16[4096,448]{1,0:T(8,128)(2,1)S(1)}, u32[]{:S(2)}) %copy-start) | copy-done | bytes 3670040
  143.7 0.1 reduce_sum.9
  143.8 0.1 reshape.214
  144.0 0.7 copy.57
  144.7 6.3 %copy.58 = bf16[1,4096,448]{1,2,0:T(8,128)(2,1)} copy(bf16[1,4096,448]{2,1,0:T(8,128)(2,1)} %bitcast.12) | data formatting | bytes 7340032
  150.9 6.3 %copy.59 = bf16[1,4096,448]{1,2,0:T(8,128)(2,1)} copy(bf16[1,4096,448]{2,1,0:T(8,128)(2,1)} %bitcast.15) | data formatting | bytes 7340032
  (17 shorter events, 0.2 us)
Async XLA Ops:
  20.8 105.3 %copy-start.1 = (bf16[128,4096]{1,0:T(8,128)(2,1)S(1)}, bf16[128,4096]{1,0:T(8,128)(2,1)}, u32[]{:S(2)}) copy-start(bf16[128,4096]{1,0:T(8,128)(2,1)} %cot_ref.1) | copy-start | bytes 3145732
  126.1 1.6 %copy-start.2 = (bf16[16,16,4096]{2,1,0:T(8,128)(2,1)S(1)}, bf16[16,16,4096]{2,1,0:T(8,128)(2,1)}, u32[]{:S(2)}) copy-start(bf16[16,16,4096]{2,1,0:T(8,128)(2,1)} %get-tuple-element.18) | copy-start | bytes 6291460
  127.7 1.6 %copy-start.3 = (bf16[16,16,4096]{2,1,0:T(8,128)(2,1)S(1)}, bf16[16,16,4096]{2,1,0:T(8,128)(2,1)}, u32[]{:S(2)}) copy-start(bf16[16,16,4096]{2,1,0:T(8,128)(2,1)} %get-tuple-element.19) | copy-start | bytes 6291460
  129.3 1.0 copy-start.4
  130.3 0.9 copy-start.5
  131.3 0.9 copy-start.6
  132.2 0.9 copy-start.7
  133.2 10.7 %copy-start.8 = (s32[1,8]{1,0:T(1,128)S(1)}, s32[1,8]{1,0:T(1,128)}, u32[]{:S(2)}) copy-start(s32[1,8]{1,0:T(1,128)} %param.11) | copy-start | bytes 100
  141.7 2.0 %copy-start = (bf16[4096,448]{1,0:T(8,128)(2,1)}, bf16[4096,448]{1,0:T(8,128)(2,1)S(1)}, u32[]{:S(2)}) copy-start(bf16[4096,448]{1,0:T(8,128)(2,1)S(1)} %get-tuple-element.27) | copy-start | bytes 11010052

commit v2 on v0

v2 whole, which is shorter than its diff:
```python
import functools

import jax
import jax.numpy as jnp
from jax import lax
from jax.experimental import pallas as pl
from jax.experimental.pallas import tpu as pltpu
from jax.sharding import PartitionSpec as P

MESH = pl.DeviceIdType.MESH
BF = jnp.bfloat16
F32 = jnp.float32

D = 4096
HID = 448
TOK = 128
EXP = 8
PL = 16
SIDE = 4
M = 4
ROWS = 16
LIVE = ROWS * PL
HALVES = 2
W = D // HALVES
Q = W // 4
H = W // 2


def dot(a, b, contract):
    return lax.dot_general(
        a, b, (((contract[0],), (contract[1],)), ((), ())), preferred_element_type=F32
    )


def iota(shape, dim):
    return lax.broadcasted_iota(jnp.int32, shape, dim)


def of_rows(expert, m, chosen_ref, gate_ref, cnt_ref):
    chosen = jnp.zeros(m.shape, F32)
    gate = jnp.zeros(m.shape, F32)
    for i in range(M):
        chosen = jnp.where(m == i, chosen_ref[i : i + 1, :].astype(F32), chosen)
        gate = jnp.where(m == i, gate_ref[i : i + 1, :].astype(F32), gate)
    here = iota(m.shape, 1) == expert
    live = here & (m < cnt_ref[...])

    def take(v, mask):
        return jnp.sum(jnp.where(mask, v, F32(0.0)), axis=1, keepdims=True)

    return take(chosen, here).astype(jnp.int32), take(gate, live), take(F32(1.0), live)


def main_kernel(
    chosen_ref, gate_ref, cnt_ref, cnt_smem, tok_hbm, cot_hbm, wg_hbm, wu_hbm, wd_hbm,
    t_out, s_out, hid_t, pgg_t, pug_t, zr_ref,
    x_in, wg, wu, wd, csend, crecv, lsend, lrecv,
    zsend, zrecv, xsend, xrecv, esend, erecv, zsback, zrback,
    tbuf, sbuf, gate_acc, up_acc, grad_acc, hid, pgg, pug, turned, po, pr, r1, r2, r3, r4, qmat, fmat,
    in_sem, w_sem, out_sem, act_sem, c_ss, c_rs, l_ss, l_rs, z_ss, z_rs, x_ss, x_rs,
    e_ss, e_rs, b_ss, b_rs, ag_ss, ag_rs, rs_ss, rs_rs,
):
    dp = lax.axis_index("dp")
    ex = lax.axis_index("expert")
    x, y = lax.rem(dp, SIDE), lax.div(dp, SIDE)
    halves = range(HALVES)

    def at_z(k):
        return lax.rem(ex + k, EXP)

    def at_p(k):
        return lax.rem(dp + k, PL)

    def each(count, body):
        def step(k, _):
            body(k)
            return 0

        lax.fori_loop(1, count, step, 0)

    loads = [
        [
            pltpu.make_async_copy(
                src.at[:, pl.ds(h * W + q * Q, Q)], x_in.at[h, a * 4 + q], in_sem.at[h, a * 4 + q]
            )
            for a, src in enumerate((tok_hbm, cot_hbm))
            for q in range(4)
        ]
        for h in halves
    ]
    for h in halves:
        for c in loads[h]:
            c.start()
    barrier = pltpu.get_barrier_semaphore()

    def greet(device):
        pl.semaphore_signal(barrier, inc=1, device_id=device, device_id_type=MESH)

    each(EXP, lambda k: greet((dp, at_z(k))))
    each(PL, lambda k: greet((at_p(k), ex)))
    wcopies = [
        pltpu.make_async_copy(src, dst, w_sem.at[i])
        for i, (src, dst) in enumerate(((wg_hbm, wg), (wu_hbm, wu), (wd_hbm, wd)))
    ]

    for e in range(EXP):
        csend[e] = jnp.full((8, 128), cnt_smem[0, e], jnp.int32)
    r = iota((256, EXP), 0)
    token, weight, _ = of_rows(r >> 5, r & 3, chosen_ref, gate_ref, cnt_ref)
    r = iota((256, 1), 0)
    token = token + (((r >> 2) & 1) * 4 + ((r >> 3) & 3)) * TOK
    weight = jnp.where((r & 4) == 0, F32(1.0), weight)
    pick = jnp.where(iota((256, 8 * TOK), 1) == token, weight, F32(0.0)).astype(BF)

    def remote(src, dst, ss, rs, device):
        return pltpu.make_async_remote_copy(
            src_ref=src, dst_ref=dst, send_sem=ss, recv_sem=rs, device_id=device,
            device_id_type=MESH,
        )

    def c_copy(k, dst):
        return remote(csend.at[at_z(k)], crecv.at[dst], c_ss.at[k], c_rs.at[k], (dp, at_z(k)))

    def z_copy(h, k, dst):
        return remote(
            zsend.at[h, at_z(k)], zrecv.at[h, dst], z_ss.at[h, k], z_rs.at[h, k], (dp, at_z(k))
        )

    def b_copy(h, k, dst):
        return remote(
            zsback.at[h, at_z(k)], zrback.at[h, dst], b_ss.at[h, k], b_rs.at[h, k], (dp, at_z(k))
        )

    def l_copy(k, dst):
        return remote(lsend, lrecv.at[dst], l_ss.at[k], l_rs.at[k], (at_p(k), ex))

    def x_copy(h, k, dst):
        return remote(
            xsend.at[h, at_p(k)], xrecv.at[h, dst], x_ss.at[h, k], x_rs.at[h, k], (at_p(k), ex)
        )

    def e_copy(h, k, dst):
        return remote(
            esend.at[h, at_p(k)], erecv.at[h, dst], e_ss.at[h, k], e_rs.at[h, k], (at_p(k), ex)
        )

    for h in halves:
        for c in loads[h]:
            c.wait()
        if h == HALVES - 1:
            for c in wcopies:
                c.start()
        zsend[h] = dot(pick, x_in[h].reshape(8 * TOK, Q), (1, 0)).astype(BF).reshape(EXP, 32, Q)
        if h == 0:
            pl.semaphore_wait(barrier, EXP - 1 + PL - 1)
            each(EXP, lambda k: c_copy(k, ex).start())
        each(EXP, lambda k, h=h: z_copy(h, k, ex).start())
        zrecv[h, ex] = zsend[h, ex]
    crecv[ex] = csend[ex]
    each(EXP, lambda k: c_copy(k, at_z(EXP - k)).wait_recv())

    total = crecv[0]
    for s in range(1, EXP):
        total = total + crecv[s]
    lsend[...] = total
    lrecv[dp] = total
    each(PL, lambda k: l_copy(k, dp).start())

    lane = iota((8, 256), 1)
    src = lane >> 5
    rank = lane & 3
    used = jnp.zeros((8, 256), jnp.int32)
    for s in range(EXP):
        v = jnp.concatenate([crecv[s], crecv[s]], axis=1)
        used = jnp.where(src == s, v, used)
        if s < EXP - 1:
            rank = rank + jnp.where(src > s, v, 0)
    alive = (lane & 3) < used

    each(PL, lambda k: l_copy(k, at_p(PL - k)).wait_recv())
    zero = jnp.zeros((8, 128), jnp.int32)
    before = zero
    col = lane >> 4
    off_l = jnp.zeros((8, 256), jnp.int32)
    len_l = jnp.zeros((8, 256), jnp.int32)
    running = zero
    for i in range(PL):
        v = lrecv[i]
        off_l = jnp.where(col == i, jnp.concatenate([running, running], axis=1), off_l)
        len_l = jnp.where(col == i, jnp.concatenate([v, v], axis=1), len_l)
        before = before + jnp.where(i < dp, v, zero)
        running = running + v
    dealt = rank + jnp.concatenate([before, before], axis=1)
    to = ((dealt & 15) << 4) + (((lane >> 3) & 3) << 2) + (((lane >> 2) & 1) << 1) + (rank >> 4)
    to = jnp.where(alive, to, -1)[0:1, :]
    qmat[...] = jnp.where(iota((256, 256), 0) == to, F32(1.0), F32(0.0)).astype(BF)
    own = ((dp - off_l + 512) & 15) + ((lane & 1) << 4)
    to = (((lane >> 1) & 1) << 6) + (((lane >> 2) & 3) << 4) + ((off_l + own) >> 4)
    to = jnp.where(own < len_l, to, -1)[0:1, :]
    fmat[...] = jnp.where(iota((128, 256), 0) == to, F32(1.0), F32(0.0)).astype(BF)

    for h in halves:
        each(EXP, lambda k, h=h: z_copy(h, k, at_z(EXP - k)).wait_recv())
        xsend[h] = (
            dot(qmat[...], zrecv[h].reshape(256, Q), (1, 0)).astype(BF).reshape(PL, ROWS, Q)
        )
        each(PL, lambda k, h=h: x_copy(h, k, dp).start())
        xrecv[h, dp] = xsend[h, dp]

    def compact(h):
        each(PL, lambda k: x_copy(h, k, at_p(PL - k)).wait_recv())
        mine = dot(fmat[...], xrecv[h].reshape(256, Q), (1, 0)).astype(BF)
        for q in range(4):
            tbuf[h, dp, :, pl.ds(q * Q, Q)] = mine[q * 16 : q * 16 + 16]
            sbuf[h, dp, :, pl.ds(q * Q, Q)] = mine[64 + q * 16 : 64 + q * 16 + 16]

    ups = [[lax.rem(v + o, SIDE) if o else v for o in range(SIDE)] for v in (x, y)]
    blocks = [[ups[1][oy] * SIDE + ups[0][ox] for ox in range(SIDE)] for oy in range(SIDE)]

    def block_of(part, ou, ov):
        ou, ov = ou % SIDE, ov % SIDE
        return blocks[ov][ou] if part == 0 else blocks[ou][ov]

    def device(part, du, dv):
        return (block_of(part, du, dv), ex)

    gathered = (tbuf, sbuf)
    sign = (1, -1)
    both = [(part, d) for part in range(2) for d in range(2)]
    sent = []

    def go(c):
        c.start()
        sent.append(c)

    def ag_steps(h):
        def ag(part, ident, block, half, du, dv):
            ref = gathered[part].at[h, block]
            if half is not None:
                ref = ref.at[:, pl.ds(half * H, H)]
            return remote(
                ref, ref, ag_ss.at[h, part, ident], ag_rs.at[h, part, ident], device(part, du, dv)
            )

        def phase2(part, o):
            for d in range(2):
                go(ag(part, 4 + o * 4 + d, block_of(part, o, 0), None, 0, sign[d]))

        def begin():
            for part in range(2):
                for d in range(2):
                    go(ag(part, d, block_of(part, 0, 0), None, sign[d], 0))
                phase2(part, 0)

        def near():
            for part, d in both:
                o = 3 if d == 0 else 1
                b = block_of(part, o, 0)
                ag(part, d, b, None, sign[d], 0).wait_recv()
                go(ag(part, 2 + d, b, d, sign[d], 0))
                phase2(part, o)

        def far():
            for part, d in both:
                ag(part, 2 + d, block_of(part, 2, 0), d, sign[d], 0).wait_recv()
            for part in range(2):
                phase2(part, 2)

        def pass_on(o):
            for part, d in both:
                b = block_of(part, o, -sign[d])
                ag(part, 4 + o * 4 + d, b, None, 0, sign[d]).wait_recv()
                go(ag(part, 4 + o * 4 + 2 + d, b, d, 0, sign[d]))

        def finish():
            for o in (0, 3, 1, 2):
                for part, d in both:
                    b = block_of(part, o, 2)
                    ag(part, 4 + o * 4 + 2 + d, b, d, 0, sign[d]).wait_recv()

        return begin, near, far, pass_on, finish

    outs = [
        [
            pltpu.make_async_copy(buf.at[h], out.at[h], out_sem.at[h, i])
            for i, (buf, out) in enumerate(((tbuf, t_out), (sbuf, s_out)))
        ]
        for h in halves
    ]

    def first(buf, w, h):
        return dot(buf[h].reshape(LIVE, W), w[:, pl.ds(h * W, W)], (1, 1))

    begin0, near0, far0, pass0, finish0 = ag_steps(0)
    begin1, near1, far1, pass1, finish1 = ag_steps(1)
    compact(0)
    begin0()
    compact(1)
    begin1()
    near0()
    pass0(0)
    far0()
    near1()
    pass0(3)
    pass0(1)
    pass1(0)
    far1()
    pass0(2)
    pass1(3)
    finish0()
    for c in outs[0]:
        c.start()
    for c in wcopies:
        c.wait()
    gate_acc[...] = first(tbuf, wg, 0)
    pass1(1)
    up_acc[...] = first(tbuf, wu, 0)
    pass1(2)
    grad_acc[...] = first(sbuf, wd, 0)
    finish1()
    for c in outs[1]:
        c.start()
    pre_gate = gate_acc[...] + first(tbuf, wg, 1)
    pre_up = up_acc[...] + first(tbuf, wu, 1)
    hidden_grad = grad_acc[...] + first(sbuf, wd, 1)
    sig = jax.nn.sigmoid(pre_gate)
    swish = pre_gate * sig
    slope = sig * (1.0 + pre_gate * (1.0 - sig))
    hid[...] = (swish * pre_up).astype(BF)
    pgg[...] = (hidden_grad * pre_up * slope).astype(BF)
    pug[...] = (hidden_grad * swish).astype(BF)

    partial = (po, pr)
    shape = (SIDE, SIDE, ROWS, Q)

    def second(h):
        def step(n, _):
            cols = pl.ds(pl.multiple_of(h * W + n * Q, Q), Q)
            to = pl.ds(pl.multiple_of(n * Q, Q), Q)
            po[h, :, :, :, to] = dot(hid[...], wd[:, cols], (1, 0)).astype(BF).reshape(shape)
            grad = dot(pgg[...], wg[:, cols], (1, 0)) + dot(pug[...], wu[:, cols], (1, 0))
            pr[h, :, :, :, to] = grad.astype(BF).reshape(shape)
            return 0

        lax.fori_loop(0, 4, step, 0)

    def cols_of(half):
        return pl.ds(half * H, H)

    def rs_steps(h):
        def group(part, ov):
            v = ups[1 - part][ov % SIDE]
            return partial[part].at[h, v] if part == 0 else partial[part].at[h, :, v]

        def piece(part, ou):
            u, v = ups[part][ou % SIDE], ups[1 - part][0]
            return partial[part].at[h, v, u] if part == 0 else partial[part].at[h, u, v]

        def rs(part, ident, src, dst, du, dv):
            return remote(
                src, dst, rs_ss.at[h, part, ident], rs_rs.at[h, part, ident], device(part, du, dv)
            )

        def far(part, d):
            src = group(part, 2).at[:, :, cols_of(d)]
            return rs(part, d, src, r1.at[h, part, d], 0, sign[d])

        def near(part, d, c):
            src = group(part, sign[d]).at[:, :, cols_of(c)]
            return rs(part, 2 + 2 * d + c, src, r2.at[h, part, d, c], 0, sign[d])

        def far_block(part, d):
            src = piece(part, 2).at[:, cols_of(d)]
            return rs(part, 6 + d, src, r3.at[h, part, d], sign[d], 0)

        def near_block(part, d, c):
            src = piece(part, sign[d]).at[:, cols_of(c)]
            return rs(part, 8 + 2 * d + c, src, r4.at[h, part, d, c], sign[d], 0)

        def begin():
            for d in range(2):
                for part in range(2):
                    go(far(part, d))
            for d in range(2):
                for part in range(2):
                    go(near(part, d, 1 - d))

        def add_far():
            for d in range(2):
                for part in range(2):
                    far(part, d).wait_recv()
                    ref = group(part, sign[d]).at[:, :, cols_of(d)]
                    ref[...] = (ref[...].astype(F32) + r1[h, part, d].astype(F32)).astype(BF)
                    go(near(part, d, d))

        def add_near():
            for part in range(2):
                for d in range(2):
                    for c in range(2):
                        near(part, d, c).wait_recv()
                for o in (2, 1, 3, 0):
                    u = ups[part][o]
                    for c in range(2):
                        ref = piece(part, o).at[:, cols_of(c)]
                        ref[...] = (
                            ref[...].astype(F32)
                            + r2[h, part, 0, c, u].astype(F32)
                            + r2[h, part, 1, c, u].astype(F32)
                        ).astype(BF)
                    if o == 2:
                        go(far_block(part, 0))
                        go(far_block(part, 1))
                    elif o != 0:
                        d = 0 if o == 1 else 1
                        go(near_block(part, d, 1 - d))

        def add_far_block():
            for part, d in both:
                far_block(part, d).wait_recv()
                ref = piece(part, sign[d]).at[:, cols_of(d)]
                ref[...] = (ref[...].astype(F32) + r3[h, part, d].astype(F32)).astype(BF)
                go(near_block(part, d, d))

        def finish():
            reduced = []
            for part in range(2):
                for c in range(2):
                    for d in range(2):
                        near_block(part, d, c).wait_recv()
                    full = (
                        piece(part, 0)[:, cols_of(c)].astype(F32)
                        + r4[h, part, 0, c].astype(F32)
                        + r4[h, part, 1, c].astype(F32)
                    ).astype(BF)
                    reduced += [full[:, :Q], full[:, Q:]]
            back = dot(fmat[...], jnp.concatenate(reduced, axis=0), (0, 0))
            esend[h] = back.astype(BF).reshape(PL, ROWS, Q)
            each(PL, lambda k: e_copy(h, k, dp).start())
            erecv[h, dp] = esend[h, dp]

        return begin, add_far, add_near, add_far_block, finish

    def to_shards(h):
        each(PL, lambda k: e_copy(h, k, at_p(PL - k)).wait_recv())
        back = dot(qmat[...], erecv[h].reshape(256, Q), (0, 0))
        zsback[h] = back.astype(BF).reshape(EXP, 32, Q)
        each(EXP, lambda k: b_copy(h, k, ex).start())
        zrback[h, ex] = zsback[h, ex]

    def at_shard(h):
        each(EXP, lambda k: b_copy(h, k, at_z(EXP - k)).wait_recv())
        zr_ref[h] = zrback[h].reshape(256, Q)

    steps = [rs_steps(h) for h in halves]
    for h in halves:
        second(h)
        steps[h][0]()
    acts = []
    for i, (src, dst) in enumerate(((hid, hid_t), (pgg, pgg_t), (pug, pug_t))):
        turned[i] = src[...].T
        acts.append(pltpu.make_async_copy(turned.at[i], dst, act_sem.at[i]))
        acts[i].start()
    steps[0][1]()
    steps[1][1]()
    steps[0][2]()
    steps[1][2]()
    steps[0][3]()
    steps[0][4]()
    steps[1][3]()
    steps[1][4]()
    for h in halves:
        to_shards(h)
    for h in halves:
        at_shard(h)

    each(EXP, lambda k: c_copy(k, ex).wait_send())
    each(PL, lambda k: l_copy(k, dp).wait_send())
    for h in halves:
        each(EXP, lambda k, h=h: z_copy(h, k, ex).wait_send())
        each(EXP, lambda k, h=h: b_copy(h, k, ex).wait_send())
        each(PL, lambda k, h=h: x_copy(h, k, dp).wait_send())
        each(PL, lambda k, h=h: e_copy(h, k, dp).wait_send())
    for c in sent:
        c.wait_send()
    for h in halves:
        for c in outs[h]:
            c.wait()
    for c in acts:
        c.wait()


def run_main(chosen, gate, counts, tokens, cotangent, wg, wu, wd):
    vmem = pl.BlockSpec(memory_space=pltpu.VMEM)
    anym = pl.BlockSpec(memory_space=pl.ANY)
    dma = pltpu.SemaphoreType.DMA

    def exchange(peers):
        return [pltpu.VMEM((HALVES, peers, 256 // peers, Q), BF)] * 2

    return pl.pallas_call(
        main_kernel,
        out_shape=(
            jax.ShapeDtypeStruct((HALVES, PL, ROWS, W), BF),
            jax.ShapeDtypeStruct((HALVES, PL, ROWS, W), BF),
            jax.ShapeDtypeStruct((HID, LIVE), BF),
            jax.ShapeDtypeStruct((HID, LIVE), BF),
            jax.ShapeDtypeStruct((HID, LIVE), BF),
            jax.ShapeDtypeStruct((HALVES, 256, Q), BF),
        ),
        in_specs=[vmem] * 3 + [pl.BlockSpec(memory_space=pltpu.SMEM)] + [anym] * 5,
        out_specs=(anym, anym, anym, anym, anym, vmem),
        scratch_shapes=[
            pltpu.VMEM((HALVES, 8, TOK, Q), BF),
            *[pltpu.VMEM((HID, D), BF)] * 3,
            pltpu.VMEM((EXP, 8, 128), jnp.int32),
            pltpu.VMEM((EXP, 8, 128), jnp.int32),
            pltpu.VMEM((8, 128), jnp.int32),
            pltpu.VMEM((PL, 8, 128), jnp.int32),
            *exchange(EXP),
            *exchange(PL),
            *exchange(PL),
            *exchange(EXP),
            *[pltpu.VMEM((HALVES, PL, ROWS, W), BF)] * 2,
            *[pltpu.VMEM((LIVE, HID), F32)] * 3,
            *[pltpu.VMEM((LIVE, HID), BF)] * 3,
            pltpu.VMEM((3, HID, LIVE), BF),
            *[pltpu.VMEM((HALVES, SIDE, SIDE, ROWS, W), BF)] * 2,
            pltpu.VMEM((HALVES, 2, 2, SIDE, ROWS, H), BF),
            pltpu.VMEM((HALVES, 2, 2, 2, SIDE, ROWS, H), BF),
            pltpu.VMEM((HALVES, 2, 2, ROWS, H), BF),
            pltpu.VMEM((HALVES, 2, 2, 2, ROWS, H), BF),
            pltpu.VMEM((256, 256), BF),
            pltpu.VMEM((128, 256), BF),
            dma((HALVES, 8)),
            dma((3,)),
            dma((HALVES, 2)),
            dma((3,)),
            *[dma((EXP,))] * 2,
            *[dma((PL,))] * 2,
            *[dma((HALVES, EXP))] * 2,
            *[dma((HALVES, PL))] * 2,
            *[dma((HALVES, PL))] * 2,
            *[dma((HALVES, EXP))] * 2,
            *[dma((HALVES, 2, 20))] * 2,
            *[dma((HALVES, 2, 12))] * 2,
        ],
        compiler_params=pltpu.CompilerParams(
            collective_id=0, has_side_effects=True, vmem_limit_bytes=58 * 1024 * 1024
        ),
        cost_estimate=pl.CostEstimate(
            flops=6 * 2 * LIVE * D * HID, bytes_accessed=20 << 20, transcendentals=LIVE * HID
        ),
        name="routed_experts",
    )(chosen, gate, counts, counts, tokens, cotangent, wg, wu, wd)


def tail_kernel(
    chosen_ref, gate_ref, cnt_ref, t_hbm, s_hbm, hid_hbm, pgg_hbm, pug_hbm, zr_hbm, cot_hbm,
    comb_out, tg_out, prob_ref, gg_out, gu_out, gd_out,
    t, s, hid, pgg, pug, zr, cot, comb, tg, gg, gu, gd, in_sem, out_sem,
):
    def load(src, dst, i):
        c = pltpu.make_async_copy(src, dst, in_sem.at[i])
        c.start()
        return c

    order = [
        [load(pgg_hbm, pgg, 0), load(t_hbm.at[0], t.at[0], 1), load(pug_hbm, pug, 2)],
        [load(hid_hbm, hid, 3), load(s_hbm.at[0], s.at[0], 4)],
        [load(zr_hbm, zr, 5), load(cot_hbm, cot, 6)],
        [load(t_hbm.at[1], t.at[1], 7), load(s_hbm.at[1], s.at[1], 8)],
    ]
    stores = []

    def store(src, dst, cols, i, n):
        c = pltpu.make_async_copy(src.at[:, cols], dst.at[:, cols], out_sem.at[i, n])
        c.start()
        stores.append(c)

    r = iota((32, EXP), 0)
    token, weight, used = of_rows(r & 7, r >> 3, chosen_ref, gate_ref, cnt_ref)
    match = iota((32, TOK), 1) == token
    pick_w = jnp.where(match, weight, F32(0.0)).astype(BF)
    pick_live = jnp.where(match, used, F32(0.0)).astype(BF)
    r = iota((64, 1), 0)
    target = ((r & 7) << 5) + ((r >> 5) << 2) + ((r >> 3) & 3)
    lane = iota((64, 256), 1)
    part = jnp.zeros((32, 128), F32)

    def wait(copies):
        for c in copies:
            c.wait()

    for n in range(D // Q):
        h, q = n // 4, n % 4
        cols = pl.ds(n * Q, Q)
        here = pl.ds(q * Q, Q)
        if n == 0:
            wait(order[0])
        elif n == 4:
            wait(order[3])
        tile = t[h, :, :, here].reshape(LIVE, Q)
        gg[:, cols] = dot(pgg[...], tile, (1, 0)).astype(BF)
        store(gg, gg_out, cols, 0, n)
        gu[:, cols] = dot(pug[...], tile, (1, 0)).astype(BF)
        store(gu, gu_out, cols, 1, n)
        if n == 0:
            wait(order[1])
        gd[:, cols] = dot(hid[...], s[h, :, :, here].reshape(LIVE, Q), (1, 0)).astype(BF)
        store(gd, gd_out, cols, 2, n)
        if n == 0:
            wait(order[2])
        pick = jnp.where(lane == target + q * 8, F32(1.0), F32(0.0)).astype(BF)
        rows = dot(pick, zr[h], (1, 0))
        out_rows = rows[:32]
        comb[:, cols] = dot(pick_w, out_rows.astype(BF), (0, 0)).astype(BF)
        store(comb, comb_out, cols, 3, n)
        tg[:, cols] = dot(pick_live, rows[32:].astype(BF), (0, 0)).astype(BF)
        store(tg, tg_out, cols, 4, n)
        prod = dot(pick_live, cot[:, cols], (1, 0)) * out_rows
        for i in range(Q // 128):
            part = part + prod[:, i * 128 : (i + 1) * 128]

    inner = jnp.sum(part, axis=1, keepdims=True)
    eye = iota((EXP, EXP), 0) == iota((EXP, EXP), 1)
    lines = [
        jnp.sum(jnp.where(eye, inner[m * EXP : (m + 1) * EXP], F32(0.0)), axis=0, keepdims=True)
        for m in range(M)
    ]
    prob_ref[...] = jnp.concatenate(lines, axis=0).astype(BF)
    wait(stores)


def run_tail(chosen, gate, counts, t, s, hid, pgg, pug, zr, cotangent):
    vmem = pl.BlockSpec(memory_space=pltpu.VMEM)
    anym = pl.BlockSpec(memory_space=pl.ANY)
    tokens = jax.ShapeDtypeStruct((TOK, D), BF)
    grads = jax.ShapeDtypeStruct((HID, D), BF)
    return pl.pallas_call(
        tail_kernel,
        out_shape=(tokens, tokens, jax.ShapeDtypeStruct((M, EXP), BF), grads, grads, grads),
        in_specs=[vmem] * 3 + [anym] * 7,
        out_specs=(anym, anym, vmem, anym, anym, anym),
        scratch_shapes=[
            *[pltpu.VMEM((HALVES, PL, ROWS, W), BF)] * 2,
            *[pltpu.VMEM((HID, LIVE), BF)] * 3,
            pltpu.VMEM((HALVES, 256, Q), BF),
            *[pltpu.VMEM((TOK, D), BF)] * 3,
            *[pltpu.VMEM((HID, D), BF)] * 3,
            pltpu.SemaphoreType.DMA((9,)),
            pltpu.SemaphoreType.DMA((5, D // Q)),
        ],
        compiler_params=pltpu.CompilerParams(vmem_limit_bytes=58 * 1024 * 1024),
        cost_estimate=pl.CostEstimate(
            flops=3 * 2 * LIVE * D * HID, bytes_accessed=20 << 20, transcendentals=0
        ),
        name="weight_grads_and_combine",
    )(chosen, gate, counts, t, s, hid, pgg, pug, zr, cotangent)


def per_device(tokens, cotangent, chosen, counts, gate_prob, w_gate, w_up, w_down):
    routes = (chosen[0].T, gate_prob[0].T, counts)
    t, s, hid, pgg, pug, zr = run_main(
        *routes, tokens, cotangent, w_gate[0].T, w_up[0].T, w_down[0]
    )
    combined, token_grad, prob_grad, gg, gu, gd = run_tail(
        *routes, t, s, hid, pgg, pug, zr, cotangent
    )
    return combined, token_grad, prob_grad.T[None], gg.T[None], gu.T[None], gd[None]


def solution(mesh):
    tokens = P(("dp", "expert"), None)
    slots = P(("dp", "expert"), None, None)
    specs = (tokens, tokens, slots, tokens, slots)
    weights = (P("expert", None, "dp"), P("expert", None, "dp"), P("expert", "dp", None))
    return jax.shard_map(
        per_device,
        mesh=mesh,
        in_specs=specs + weights,
        out_specs=(tokens, tokens, slots) + weights,
        check_vma=False,
    )
```

time: 343 us -> 113 us (0.33)
  waiting for transfers between devices: 186 us -> 0 us
  Pallas kernels: 0 us -> 112 us
  blocking collectives: 57 us -> 0 us
  matrix products: 55.1 us -> 0 us
  starting transfers between devices: 17.6 us -> 0 us
  between operations: 14.6 us -> 0.8 us
  local copies, waits for them, and re-layouts: 11.8 us -> 0 us
    reduce_scatter x2 -> x0, waiting for transfers between devices: 139 us -> none  [the longest x1 72.6 us: per_device(): lax.psum_scatter(grad_parts, 'dp', scatter_dimension=1, tiled=True)]
    pallas_call x0 -> x2, Pallas kernels: none -> 112 us  [the longest x1 102 us: run_main(): pl.pallas_call(main_kernel, out_shape=(jax.ShapeDtypeStruct((HALVES, PL,...]
    dot_general x11 -> x0, matrix products: 55.1 us -> none  [the longest x1 6.22 us: expert_pass(): lax.dot_general(hidden, scaled, (((0,), (0,)), ((), ())), preferred_eleme...]
    all_gather x2 -> x0, waiting for transfers between devices: 41.6 us -> none  [the longest x1 41.6 us: per_device(): lax.all_gather(part_cot, 'dp', axis=1, tiled=True)]
    unnamed x1 -> x0, blocking collectives: 33.9 us -> none
    all_to_all x2 -> x0, blocking collectives: 23.1 us -> none  [the longest x1 13.1 us: per_device(): lax.all_to_all(sent_tokens, 'expert', split_axis=0, concat_axis=1, tiled=...]
    all_to_all x3 -> x0, starting transfers between devices: 17.3 us -> none  [the longest x1 6.55 us: send_back(): lax.all_to_all(reduced_grad, 'expert', split_axis=1, concat_axis=0, tiled...]
    all_to_all x3 -> x0, waiting for transfers between devices: 5.33 us -> none  [the longest x1 3.27 us: per_device(): lax.all_to_all(weights, 'expert', split_axis=0, concat_axis=1, tiled=True)]
  transfers between devices with their start and end apart: 7 -> 0, of which waited for: 5 -> 0; matrix products, arithmetic and copies ran while one was open for 14% -> 0% of each run, Pallas kernels for 0% -> 0%
where the time goes in v2:
time: 113 us
  Pallas kernels  112 us (99%)
    pallas_call x1, Pallas kernels, run_main(): pl.pallas_call(main_kernel, out_shape=(jax.ShapeDtypeStruct((HALVES, PL,...  102 us
    pallas_call x1, Pallas kernels, run_tail(): pl.pallas_call(tail_kernel, out_shape=(tokens, tokens, jax.ShapeDtypeStru...  9.54 us

profile of v2, /device:TPU:1, one launch (start us, length us, event | category | flops | bytes accessed | tf_op | source)
XLA Modules:
  0.0 112.6 jit_solution(15122021387843457976)
XLA Ops:
  0.6 102.2 %routed_experts.1 = (bf16[2,16,16,2048]{3,2,1,0:T(8,128)(2,1)}, bf16[2,16,16,2048]{3,2,1,0:T(8,128)(2,1)}, bf16[448,256]{1,0:T(8,128)(2,1)}, bf16[448,256]{1,0:T...) custom-call(s32[4,8]{1,0:T(4,128)} %bitcast.26, bf16[4,8]{1,0:T(4,128)(2,1)} %bitcast.28, ...), custom_call_target="tpu_custom_call" | custom-call | flops 5637144576 | bytes 20971520 | tf_op jit(solution)/shard_map/routed_experts/pallas_call | solution.py:500
  102.9 9.5 %weight_grads_and_combine.1 = (bf16[128,4096]{1,0:T(8,128)(2,1)}, bf16[128,4096]{1,0:T(8,128)(2,1)}, bf16[4,8]{1,0:T(4,128)(2,1)}, bf16[448,4096]{1,0:T(8,128)(2...) custom-call(s32[4,8]{1,0:T(4,128)} %bitcast.27, bf16[4,8]{1,0:T(4,128)(2,1)} %bitcast.29, s32[1,8]{1,0:T(1,128)} %cnt_ref.3, ...), custom_call_target="tpu_custom_call" | custom-call | flops 2818572288 | bytes 20971520 | tf_op jit(solution)/shard_map/weight_grads_and_combine/pallas_call | solution.py:639

commit v3 on v2

--- a/solution.py
+++ b/solution.py
@@ -20,10 +20,20 @@
 M = 4
 ROWS = 16
 LIVE = ROWS * PL
-HALVES = 2
-W = D // HALVES
+CHUNKS = 2
+W = D // CHUNKS
+TILE = 512
+AG_LAG, RS_LAG = 2, 1
 Q = W // 4
 H = W // 2
+
+
+def interleave(chunks, lag, newest_first):
+    count = len(chunks[0]) + lag * (len(chunks) - 1)
+    for t in range(count):
+        for c in reversed(range(len(chunks))) if newest_first else range(len(chunks)):
+            if 0 <= t - lag * c < len(chunks[c]):
+                chunks[c][t - lag * c]()
 
 
 def dot(a, b, contract):
@@ -53,17 +63,17 @@
 
 def main_kernel(
     chosen_ref, gate_ref, cnt_ref, cnt_smem, tok_hbm, cot_hbm, wg_hbm, wu_hbm, wd_hbm,
-    t_out, s_out, hid_t, pgg_t, pug_t, zr_ref,
+    t_out, s_out, hid_t, pgg_t, pug_t, zr_out,
     x_in, wg, wu, wd, csend, crecv, lsend, lrecv,
-    zsend, zrecv, xsend, xrecv, esend, erecv, zsback, zrback,
+    zsend, zrecv, xsend, xrecv, esend, erecv, zsback,
     tbuf, sbuf, gate_acc, up_acc, grad_acc, hid, pgg, pug, turned, po, pr, r1, r2, r3, r4, qmat, fmat,
-    in_sem, w_sem, out_sem, act_sem, c_ss, c_rs, l_ss, l_rs, z_ss, z_rs, x_ss, x_rs,
+    in_sem, w_sem, out_sem, act_sem, keep_sem, c_ss, c_rs, l_ss, l_rs, z_ss, z_rs, x_ss, x_rs,
     e_ss, e_rs, b_ss, b_rs, ag_ss, ag_rs, rs_ss, rs_rs,
 ):
     dp = lax.axis_index("dp")
     ex = lax.axis_index("expert")
     x, y = lax.rem(dp, SIDE), lax.div(dp, SIDE)
-    halves = range(HALVES)
+    chunks = range(CHUNKS)
 
     def at_z(k):
         return lax.rem(ex + k, EXP)
@@ -86,9 +96,9 @@
             for a, src in enumerate((tok_hbm, cot_hbm))
             for q in range(4)
         ]
-        for h in halves
+        for h in chunks
     ]
-    for h in halves:
+    for h in chunks:
         for c in loads[h]:
             c.start()
     barrier = pltpu.get_barrier_semaphore()
@@ -128,8 +138,11 @@
 
     def b_copy(h, k, dst):
         return remote(
-            zsback.at[h, at_z(k)], zrback.at[h, dst], b_ss.at[h, k], b_rs.at[h, k], (dp, at_z(k))
+            zsback.at[h, at_z(k)], zr_out.at[h, dst], b_ss.at[h, k], b_rs.at[h, k], (dp, at_z(k))
         )
+
+    def keep(h):
+        return pltpu.make_async_copy(zsback.at[h, ex], zr_out.at[h, ex], keep_sem.at[h])
 
     def l_copy(k, dst):
         return remote(lsend, lrecv.at[dst], l_ss.at[k], l_rs.at[k], (at_p(k), ex))
@@ -144,10 +157,10 @@
             esend.at[h, at_p(k)], erecv.at[h, dst], e_ss.at[h, k], e_rs.at[h, k], (at_p(k), ex)
         )
 
-    for h in halves:
+    for h in chunks:
         for c in loads[h]:
             c.wait()
-        if h == HALVES - 1:
+        if h == CHUNKS - 1:
             for c in wcopies:
                 c.start()
         zsend[h] = dot(pick, x_in[h].reshape(8 * TOK, Q), (1, 0)).astype(BF).reshape(EXP, 32, Q)
@@ -199,7 +212,7 @@
     to = jnp.where(own < len_l, to, -1)[0:1, :]
     fmat[...] = jnp.where(iota((128, 256), 0) == to, F32(1.0), F32(0.0)).astype(BF)
 
-    for h in halves:
+    for h in chunks:
         each(EXP, lambda k, h=h: z_copy(h, k, at_z(EXP - k)).wait_recv())
         xsend[h] = (
             dot(qmat[...], zrecv[h].reshape(256, Q), (1, 0)).astype(BF).reshape(PL, ROWS, Q)
@@ -247,9 +260,9 @@
                 go(ag(part, 4 + o * 4 + d, block_of(part, o, 0), None, 0, sign[d]))
 
         def begin():
+            for part, d in both:
+                go(ag(part, d, block_of(part, 0, 0), None, sign[d], 0))
             for part in range(2):
-                for d in range(2):
-                    go(ag(part, d, block_of(part, 0, 0), None, sign[d], 0))
                 phase2(part, 0)
 
         def near():
@@ -258,7 +271,8 @@
                 b = block_of(part, o, 0)
                 ag(part, d, b, None, sign[d], 0).wait_recv()
                 go(ag(part, 2 + d, b, d, sign[d], 0))
-                phase2(part, o)
+            for part, d in both:
+                phase2(part, 3 if d == 0 else 1)
 
         def far():
             for part, d in both:
@@ -285,64 +299,73 @@
             pltpu.make_async_copy(buf.at[h], out.at[h], out_sem.at[h, i])
             for i, (buf, out) in enumerate(((tbuf, t_out), (sbuf, s_out)))
         ]
-        for h in halves
+        for h in chunks
     ]
 
     def first(buf, w, h):
         return dot(buf[h].reshape(LIVE, W), w[:, pl.ds(h * W, W)], (1, 1))
 
-    begin0, near0, far0, pass0, finish0 = ag_steps(0)
-    begin1, near1, far1, pass1, finish1 = ag_steps(1)
-    compact(0)
-    begin0()
-    compact(1)
-    begin1()
-    near0()
-    pass0(0)
-    far0()
-    near1()
-    pass0(3)
-    pass0(1)
-    pass1(0)
-    far1()
-    pass0(2)
-    pass1(3)
-    finish0()
-    for c in outs[0]:
-        c.start()
-    for c in wcopies:
-        c.wait()
-    gate_acc[...] = first(tbuf, wg, 0)
-    pass1(1)
-    up_acc[...] = first(tbuf, wu, 0)
-    pass1(2)
-    grad_acc[...] = first(sbuf, wd, 0)
-    finish1()
-    for c in outs[1]:
-        c.start()
-    pre_gate = gate_acc[...] + first(tbuf, wg, 1)
-    pre_up = up_acc[...] + first(tbuf, wu, 1)
-    hidden_grad = grad_acc[...] + first(sbuf, wd, 1)
+    def gather_steps(h):
+        begin, near, far, pass_on, finish = ag_steps(h)
+
+        def start():
+            compact(h)
+            begin()
+
+        def end():
+            finish()
+            for c in outs[h]:
+                c.start()
+            if h == 0:
+                for c in wcopies:
+                    c.wait()
+
+        def add(acc, buf, w):
+            acc[...] = first(buf, w, h) if h == 0 else acc[...] + first(buf, w, h)
+
+        return [
+            start,
+            near,
+            lambda: pass_on(0),
+            far,
+            lambda: pass_on(3),
+            lambda: pass_on(1),
+            lambda: pass_on(2),
+            end,
+            lambda: add(gate_acc, tbuf, wg),
+            lambda: add(up_acc, tbuf, wu),
+            lambda: add(grad_acc, sbuf, wd) if h < CHUNKS - 1 else None,
+        ]
+
+    interleave([gather_steps(h) for h in chunks], AG_LAG, False)
+    pre_gate = gate_acc[...]
+    pre_up = up_acc[...]
     sig = jax.nn.sigmoid(pre_gate)
     swish = pre_gate * sig
-    slope = sig * (1.0 + pre_gate * (1.0 - sig))
     hid[...] = (swish * pre_up).astype(BF)
-    pgg[...] = (hidden_grad * pre_up * slope).astype(BF)
-    pug[...] = (hidden_grad * swish).astype(BF)
+    gate_acc[...] = swish
+    up_acc[...] = pre_up * (sig * (1.0 + pre_gate * (1.0 - sig)))
+
+    def hidden_grads():
+        hidden_grad = grad_acc[...] + first(sbuf, wd, CHUNKS - 1)
+        pgg[...] = (hidden_grad * up_acc[...]).astype(BF)
+        pug[...] = (hidden_grad * gate_acc[...]).astype(BF)
 
     partial = (po, pr)
-    shape = (SIDE, SIDE, ROWS, Q)
-
-    def second(h):
+    shape = (SIDE, SIDE, ROWS, TILE)
+
+    def second(h, part, half):
         def step(n, _):
-            cols = pl.ds(pl.multiple_of(h * W + n * Q, Q), Q)
-            to = pl.ds(pl.multiple_of(n * Q, Q), Q)
-            po[h, :, :, :, to] = dot(hid[...], wd[:, cols], (1, 0)).astype(BF).reshape(shape)
-            grad = dot(pgg[...], wg[:, cols], (1, 0)) + dot(pug[...], wu[:, cols], (1, 0))
-            pr[h, :, :, :, to] = grad.astype(BF).reshape(shape)
+            cols = pl.ds(pl.multiple_of(h * W + n * TILE, TILE), TILE)
+            to = pl.ds(pl.multiple_of(n * TILE, TILE), TILE)
+            if part == 0:
+                sums = dot(hid[...], wd[:, cols], (1, 0))
+            else:
+                sums = dot(pgg[...], wg[:, cols], (1, 0)) + dot(pug[...], wu[:, cols], (1, 0))
+            partial[part][h, :, :, :, to] = sums.astype(BF).reshape(shape)
             return 0
 
-        lax.fori_loop(0, 4, step, 0)
+        lax.fori_loop(half * H // TILE, (half + 1) * H // TILE, step, 0)
 
     def cols_of(half):
         return pl.ds(half * H, H)
@@ -369,21 +392,19 @@
             src = group(part, sign[d]).at[:, :, cols_of(c)]
             return rs(part, 2 + 2 * d + c, src, r2.at[h, part, d, c], 0, sign[d])
 
-        def far_block(part, d):
-            src = piece(part, 2).at[:, cols_of(d)]
-            return rs(part, 6 + d, src, r3.at[h, part, d], sign[d], 0)
-
-        def near_block(part, d, c):
-            src = piece(part, sign[d]).at[:, cols_of(c)]
-            return rs(part, 8 + 2 * d + c, src, r4.at[h, part, d, c], sign[d], 0)
-
-        def begin():
-            for d in range(2):
-                for part in range(2):
-                    go(far(part, d))
-            for d in range(2):
-                for part in range(2):
-                    go(near(part, d, 1 - d))
+        def far_block(part):
+            src = piece(part, 2)
+            return rs(part, 6, src, r3.at[h, part], 2, 0)
+
+        def near_block(part, d):
+            src = piece(part, sign[d])
+            return rs(part, 7 + d, src, r4.at[h, part, d], sign[d], 0)
+
+        def begin(part):
+            for c in range(2):
+                second(h, part, c)
+                go(far(part, c))
+                go(near(part, 1 - c, c))
 
         def add_far():
             for d in range(2):
@@ -408,81 +429,84 @@
                             + r2[h, part, 1, c, u].astype(F32)
                         ).astype(BF)
                     if o == 2:
-                        go(far_block(part, 0))
-                        go(far_block(part, 1))
+                        go(far_block(part))
                     elif o != 0:
-                        d = 0 if o == 1 else 1
-                        go(near_block(part, d, 1 - d))
-
-        def add_far_block():
-            for part, d in both:
-                far_block(part, d).wait_recv()
-                ref = piece(part, sign[d]).at[:, cols_of(d)]
-                ref[...] = (ref[...].astype(F32) + r3[h, part, d].astype(F32)).astype(BF)
-                go(near_block(part, d, d))
+                        go(near_block(part, 0 if o == 1 else 1))
 
         def finish():
             reduced = []
             for part in range(2):
-                for c in range(2):
-                    for d in range(2):
-                        near_block(part, d, c).wait_recv()
-                    full = (
-                        piece(part, 0)[:, cols_of(c)].astype(F32)
-                        + r4[h, part, 0, c].astype(F32)
-                        + r4[h, part, 1, c].astype(F32)
-                    ).astype(BF)
-                    reduced += [full[:, :Q], full[:, Q:]]
+                for d in range(2):
+                    near_block(part, d).wait_recv()
+                far_block(part).wait_recv()
+                for q in range(4):
+                    cols = pl.ds(q * Q, Q)
+                    reduced.append(
+                        (
+                            piece(part, 0)[:, cols].astype(F32)
+                            + r4[h, part, 0, :, cols].astype(F32)
+                            + r4[h, part, 1, :, cols].astype(F32)
+                            + r3[h, part, :, cols].astype(F32)
+                        ).astype(BF)
+                    )
             back = dot(fmat[...], jnp.concatenate(reduced, axis=0), (0, 0))
             esend[h] = back.astype(BF).reshape(PL, ROWS, Q)
             each(PL, lambda k: e_copy(h, k, dp).start())
             erecv[h, dp] = esend[h, dp]
 
-        return begin, add_far, add_near, add_far_block, finish
+        return begin, add_far, add_near, finish
 
     def to_shards(h):
         each(PL, lambda k: e_copy(h, k, at_p(PL - k)).wait_recv())
         back = dot(qmat[...], erecv[h].reshape(256, Q), (0, 0))
         zsback[h] = back.astype(BF).reshape(EXP, 32, Q)
         each(EXP, lambda k: b_copy(h, k, ex).start())
-        zrback[h, ex] = zsback[h, ex]
+        keep(h).start()
 
     def at_shard(h):
         each(EXP, lambda k: b_copy(h, k, at_z(EXP - k)).wait_recv())
-        zr_ref[h] = zrback[h].reshape(256, Q)
-
-    steps = [rs_steps(h) for h in halves]
-    for h in halves:
-        second(h)
-        steps[h][0]()
+        keep(h).wait()
+
     acts = []
-    for i, (src, dst) in enumerate(((hid, hid_t), (pgg, pgg_t), (pug, pug_t))):
-        turned[i] = src[...].T
-        acts.append(pltpu.make_async_copy(turned.at[i], dst, act_sem.at[i]))
-        acts[i].start()
-    steps[0][1]()
-    steps[1][1]()
-    steps[0][2]()
-    steps[1][2]()
-    steps[0][3]()
-    steps[0][4]()
-    steps[1][3]()
-    steps[1][4]()
-    for h in halves:
-        to_shards(h)
-    for h in halves:
-        at_shard(h)
+
+    def turn():
+        for i, (src, dst) in enumerate(((hid, hid_t), (pgg, pgg_t), (pug, pug_t))):
+            turned[i] = src[...].T
+            acts.append(pltpu.make_async_copy(turned.at[i], dst, act_sem.at[i]))
+            acts[i].start()
+
+    def reduce_steps(h):
+        begin, add_far, add_near, finish = rs_steps(h)
+
+        def start():
+            begin(0)
+            if h == 0:
+                hidden_grads()
+            begin(1)
+            if h == CHUNKS - 1:
+                turn()
+
+        return [
+            start,
+            add_far,
+            add_near,
+            finish,
+            lambda: to_shards(h),
+            lambda: at_shard(h),
+        ]
+
+    interleave([reduce_steps(h) for h in chunks], RS_LAG, True)
 
     each(EXP, lambda k: c_copy(k, ex).wait_send())
     each(PL, lambda k: l_copy(k, dp).wait_send())
-    for h in halves:
+    for h in chunks:
         each(EXP, lambda k, h=h: z_copy(h, k, ex).wait_send())
         each(EXP, lambda k, h=h: b_copy(h, k, ex).wait_send())
         each(PL, lambda k, h=h: x_copy(h, k, dp).wait_send())
         each(PL, lambda k, h=h: e_copy(h, k, dp).wait_send())
     for c in sent:
         c.wait_send()
-    for h in halves:
+    for h in chunks:
         for c in outs[h]:
             c.wait()
     for c in acts:
@@ -495,22 +519,22 @@
     dma = pltpu.SemaphoreType.DMA
 
     def exchange(peers):
-        return [pltpu.VMEM((HALVES, peers, 256 // peers, Q), BF)] * 2
+        return [pltpu.VMEM((CHUNKS, peers, 256 // peers, Q), BF)] * 2
 
     return pl.pallas_call(
         main_kernel,
         out_shape=(
-            jax.ShapeDtypeStruct((HALVES, PL, ROWS, W), BF),
-            jax.ShapeDtypeStruct((HALVES, PL, ROWS, W), BF),
+            jax.ShapeDtypeStruct((CHUNKS, PL, ROWS, W), BF),
+            jax.ShapeDtypeStruct((CHUNKS, PL, ROWS, W), BF),
             jax.ShapeDtypeStruct((HID, LIVE), BF),
             jax.ShapeDtypeStruct((HID, LIVE), BF),
             jax.ShapeDtypeStruct((HID, LIVE), BF),
-            jax.ShapeDtypeStruct((HALVES, 256, Q), BF),
+            jax.ShapeDtypeStruct((CHUNKS, EXP, 32, Q), BF),
         ),
         in_specs=[vmem] * 3 + [pl.BlockSpec(memory_space=pltpu.SMEM)] + [anym] * 5,
-        out_specs=(anym, anym, anym, anym, anym, vmem),
+        out_specs=(anym,) * 6,
         scratch_shapes=[
-            pltpu.VMEM((HALVES, 8, TOK, Q), BF),
+            pltpu.VMEM((CHUNKS, 8, TOK, Q), BF),
             *[pltpu.VMEM((HID, D), BF)] * 3,
             pltpu.VMEM((EXP, 8, 128), jnp.int32),
             pltpu.VMEM((EXP, 8, 128), jnp.int32),
@@ -519,30 +543,31 @@
             *exchange(EXP),
             *exchange(PL),
             *exchange(PL),
-            *exchange(EXP),
-            *[pltpu.VMEM((HALVES, PL, ROWS, W), BF)] * 2,
+            exchange(EXP)[0],
+            *[pltpu.VMEM((CHUNKS, PL, ROWS, W), BF)] * 2,
             *[pltpu.VMEM((LIVE, HID), F32)] * 3,
             *[pltpu.VMEM((LIVE, HID), BF)] * 3,
             pltpu.VMEM((3, HID, LIVE), BF),
-            *[pltpu.VMEM((HALVES, SIDE, SIDE, ROWS, W), BF)] * 2,
-            pltpu.VMEM((HALVES, 2, 2, SIDE, ROWS, H), BF),
-            pltpu.VMEM((HALVES, 2, 2, 2, SIDE, ROWS, H), BF),
-            pltpu.VMEM((HALVES, 2, 2, ROWS, H), BF),
-            pltpu.VMEM((HALVES, 2, 2, 2, ROWS, H), BF),
+            *[pltpu.VMEM((CHUNKS, SIDE, SIDE, ROWS, W), BF)] * 2,
+            pltpu.VMEM((CHUNKS, 2, 2, SIDE, ROWS, H), BF),
+            pltpu.VMEM((CHUNKS, 2, 2, 2, SIDE, ROWS, H), BF),
+            pltpu.VMEM((CHUNKS, 2, ROWS, W), BF),
+            pltpu.VMEM((CHUNKS, 2, 2, ROWS, W), BF),
             pltpu.VMEM((256, 256), BF),
             pltpu.VMEM((128, 256), BF),
-            dma((HALVES, 8)),
+            dma((CHUNKS, 8)),
             dma((3,)),
-            dma((HALVES, 2)),
+            dma((CHUNKS, 2)),
             dma((3,)),
+            dma((CHUNKS,)),
             *[dma((EXP,))] * 2,
             *[dma((PL,))] * 2,
-            *[dma((HALVES, EXP))] * 2,
-            *[dma((HALVES, PL))] * 2,
-            *[dma((HALVES, PL))] * 2,
-            *[dma((HALVES, EXP))] * 2,
-            *[dma((HALVES, 2, 20))] * 2,
-            *[dma((HALVES, 2, 12))] * 2,
+            *[dma((CHUNKS, EXP))] * 2,
+            *[dma((CHUNKS, PL))] * 2,
+            *[dma((CHUNKS, PL))] * 2,
+            *[dma((CHUNKS, EXP))] * 2,
+            *[dma((CHUNKS, 2, 20))] * 2,
+            *[dma((CHUNKS, 2, 9))] * 2,
         ],
         compiler_params=pltpu.CompilerParams(
             collective_id=0, has_side_effects=True, vmem_limit_bytes=58 * 1024 * 1024
@@ -568,7 +593,10 @@
         [load(pgg_hbm, pgg, 0), load(t_hbm.at[0], t.at[0], 1), load(pug_hbm, pug, 2)],
         [load(hid_hbm, hid, 3), load(s_hbm.at[0], s.at[0], 4)],
         [load(zr_hbm, zr, 5), load(cot_hbm, cot, 6)],
-        [load(t_hbm.at[1], t.at[1], 7), load(s_hbm.at[1], s.at[1], 8)],
+    ]
+    later = [
+        [load(t_hbm.at[h], t.at[h], 5 + 2 * h), load(s_hbm.at[h], s.at[h], 6 + 2 * h)]
+        for h in range(1, CHUNKS)
     ]
     stores = []
 
@@ -591,34 +619,37 @@
         for c in copies:
             c.wait()
 
-    for n in range(D // Q):
-        h, q = n // 4, n % 4
-        cols = pl.ds(n * Q, Q)
-        here = pl.ds(q * Q, Q)
+    for n in range(D // TILE):
+        h, at = n * TILE // W, n * TILE % W
+        cols = pl.ds(n * TILE, TILE)
+        here = pl.ds(at, TILE)
         if n == 0:
             wait(order[0])
-        elif n == 4:
-            wait(order[3])
-        tile = t[h, :, :, here].reshape(LIVE, Q)
+        elif at == 0:
+            wait(later[h - 1])
+        tile = t[h, :, :, here].reshape(LIVE, TILE)
         gg[:, cols] = dot(pgg[...], tile, (1, 0)).astype(BF)
         store(gg, gg_out, cols, 0, n)
         gu[:, cols] = dot(pug[...], tile, (1, 0)).astype(BF)
         store(gu, gu_out, cols, 1, n)
         if n == 0:
             wait(order[1])
-        gd[:, cols] = dot(hid[...], s[h, :, :, here].reshape(LIVE, Q), (1, 0)).astype(BF)
+        gd[:, cols] = dot(hid[...], s[h, :, :, here].reshape(LIVE, TILE), (1, 0)).astype(BF)
         store(gd, gd_out, cols, 2, n)
         if n == 0:
             wait(order[2])
-        pick = jnp.where(lane == target + q * 8, F32(1.0), F32(0.0)).astype(BF)
-        rows = dot(pick, zr[h], (1, 0))
+        pieces = []
+        for q in range(at // Q, (at + TILE) // Q):
+            pick = jnp.where(lane == target + q * 8, F32(1.0), F32(0.0)).astype(BF)
+            pieces.append(dot(pick, zr[h], (1, 0)))
+        rows = jnp.concatenate(pieces, axis=1) if len(pieces) > 1 else pieces[0]
         out_rows = rows[:32]
         comb[:, cols] = dot(pick_w, out_rows.astype(BF), (0, 0)).astype(BF)
         store(comb, comb_out, cols, 3, n)
         tg[:, cols] = dot(pick_live, rows[32:].astype(BF), (0, 0)).astype(BF)
         store(tg, tg_out, cols, 4, n)
         prod = dot(pick_live, cot[:, cols], (1, 0)) * out_rows
-        for i in range(Q // 128):
+        for i in range(TILE // 128):
             part = part + prod[:, i * 128 : (i + 1) * 128]
 
     inner = jnp.sum(part, axis=1, keepdims=True)
@@ -642,13 +673,13 @@
         in_specs=[vmem] * 3 + [anym] * 7,
         out_specs=(anym, anym, vmem, anym, anym, anym),
         scratch_shapes=[
-            *[pltpu.VMEM((HALVES, PL, ROWS, W), BF)] * 2,
+            *[pltpu.VMEM((CHUNKS, PL, ROWS, W), BF)] * 2,
             *[pltpu.VMEM((HID, LIVE), BF)] * 3,
-            pltpu.VMEM((HALVES, 256, Q), BF),
+            pltpu.VMEM((CHUNKS, 256, Q), BF),
             *[pltpu.VMEM((TOK, D), BF)] * 3,
             *[pltpu.VMEM((HID, D), BF)] * 3,
-            pltpu.SemaphoreType.DMA((9,)),
-            pltpu.SemaphoreType.DMA((5, D // Q)),
+            pltpu.SemaphoreType.DMA((5 + 2 * CHUNKS,)),
+            pltpu.SemaphoreType.DMA((5, D // TILE)),
         ],
         compiler_params=pltpu.CompilerParams(vmem_limit_bytes=58 * 1024 * 1024),
         cost_estimate=pl.CostEstimate(
@@ -664,7 +695,7 @@
         *routes, tokens, cotangent, w_gate[0].T, w_up[0].T, w_down[0]
     )
     combined, token_grad, prob_grad, gg, gu, gd = run_tail(
-        *routes, t, s, hid, pgg, pug, zr, cotangent
+        *routes, t, s, hid, pgg, pug, zr.reshape(CHUNKS, 256, Q), cotangent
     )
     return combined, token_grad, prob_grad.T[None], gg.T[None], gu.T[None], gd[None]
 

time: 113 us -> 108 us (0.956)
  Pallas kernels: 112 us -> 107 us
    pallas_call x1, Pallas kernels: 102 us -> 97.2 us  [run_main(): pl.pallas_call(main_kernel, out_shape=(jax.ShapeDtypeStruct((CHUNKS, PL,...]
where the time goes in v3:
time: 108 us
  Pallas kernels  107 us (99%)
    pallas_call x1, Pallas kernels, run_main(): pl.pallas_call(main_kernel, out_shape=(jax.ShapeDtypeStruct((CHUNKS, PL,...  97.2 us
    pallas_call x1, Pallas kernels, run_tail(): pl.pallas_call(tail_kernel, out_shape=(tokens, tokens, jax.ShapeDtypeStru...  9.55 us

profile of v3, /device:TPU:1, one launch (start us, length us, event | category | flops | bytes accessed | tf_op | source)
XLA Modules:
  0.0 107.5 jit_solution(16339400449957256238)
XLA Ops:
  0.6 97.2 %routed_experts.1 = (bf16[2,16,16,2048]{3,2,1,0:T(8,128)(2,1)}, bf16[2,16,16,2048]{3,2,1,0:T(8,128)(2,1)}, bf16[448,256]{1,0:T(8,128)(2,1)}, bf16[448,256]{1,0:T...) custom-call(s32[4,8]{1,0:T(4,128)} %bitcast.27, bf16[4,8]{1,0:T(4,128)(2,1)} %bitcast.29, ...), custom_call_target="tpu_custom_call" | custom-call | flops 5637144576 | bytes 20971520 | tf_op jit(solution)/shard_map/routed_experts/pallas_call | solution.py:524
  97.8 9.5 %weight_grads_and_combine.1 = (bf16[128,4096]{1,0:T(8,128)(2,1)}, bf16[128,4096]{1,0:T(8,128)(2,1)}, bf16[4,8]{1,0:T(4,128)(2,1)}, bf16[448,4096]{1,0:T(8,128)(2...) custom-call(s32[4,8]{1,0:T(4,128)} %bitcast.28, bf16[4,8]{1,0:T(4,128)(2,1)} %bitcast.30, s32[1,8]{1,0:T(1,128)} %cnt_ref.3, ...), custom_call_target="tpu_custom_call" | custom-call | flops 2818572288 | bytes 20971520 | tf_op jit(solution)/shard_map/weight_grads_and_combine/pallas_call | solution.py:670

commit v4 on v3

--- a/solution.py
+++ b/solution.py
@@ -23,7 +23,7 @@
 CHUNKS = 2
 W = D // CHUNKS
 TILE = 512
-AG_LAG, RS_LAG = 2, 1
+AG_LAG, RS_LAG = 3, 1
 Q = W // 4
 H = W // 2
 
@@ -483,12 +483,14 @@
             if h == 0:
                 hidden_grads()
             begin(1)
+        def middle():
+            add_far()
             if h == CHUNKS - 1:
                 turn()
 
         return [
             start,
-            add_far,
+            middle,
             add_near,
             finish,
             lambda: to_shards(h),

time: 108 us -> 107 us (level)
  no operation moved by 1% of the time
where the time goes in v4:
time: 107 us
  Pallas kernels  106 us (99%)
    pallas_call x1, Pallas kernels, run_main(): pl.pallas_call(main_kernel, out_shape=(jax.ShapeDtypeStruct((CHUNKS, PL,...  96.4 us
    pallas_call x1, Pallas kernels, run_tail(): pl.pallas_call(tail_kernel, out_shape=(tokens, tokens, jax.ShapeDtypeStru...  9.54 us

profile of v4, /device:TPU:1, one launch (start us, length us, event | category | flops | bytes accessed | tf_op | source)
XLA Modules:
  0.0 106.8 jit_solution(16176026589567942167)
XLA Ops:
  0.6 96.4 %routed_experts.1 = (bf16[2,16,16,2048]{3,2,1,0:T(8,128)(2,1)}, bf16[2,16,16,2048]{3,2,1,0:T(8,128)(2,1)}, bf16[448,256]{1,0:T(8,128)(2,1)}, bf16[448,256]{1,0:T...) custom-call(s32[4,8]{1,0:T(4,128)} %bitcast.27, bf16[4,8]{1,0:T(4,128)(2,1)} %bitcast.29, ...), custom_call_target="tpu_custom_call" | custom-call | flops 5637144576 | bytes 20971520 | tf_op jit(solution)/shard_map/routed_experts/pallas_call | solution.py:526
  97.1 9.5 %weight_grads_and_combine.1 = (bf16[128,4096]{1,0:T(8,128)(2,1)}, bf16[128,4096]{1,0:T(8,128)(2,1)}, bf16[4,8]{1,0:T(4,128)(2,1)}, bf16[448,4096]{1,0:T(8,128)(2...) custom-call(s32[4,8]{1,0:T(4,128)} %bitcast.28, bf16[4,8]{1,0:T(4,128)(2,1)} %bitcast.30, s32[1,8]{1,0:T(1,128)} %cnt_ref.3, ...), custom_call_target="tpu_custom_call" | custom-call | flops 2818572288 | bytes 20971520 | tf_op jit(solution)/shard_map/weight_grads_and_combine/pallas_call | solution.py:672
